TPU v7x, 128 devices: a whole 4x4x4 slice. The times are simulated.
128 devices in a mesh: ty: 16 (over z, y_lo, core), tx: 8 (over x, y_hi).
Axes of the slice: x: 4, y: 4 (y_hi: 2, y_lo: 2; y = y_hi * 2 + y_lo), z: 4, core: 2. Of those that a mesh axis runs over, the one named last changes fastest.
Arguments:
- object_field: float32 [2, 8192, 4096], P(None, 'ty', 'tx'), may hold values from -6 to 6
- probe: float32 [2, 256, 256], replicated, may hold values from -3 to 3
- measured: float32 [2048, 256, 256], P(('ty', 'tx')), may hold values from 0.1 to 4
- offsets: int32 [2048, 2], P(('ty', 'tx')), may hold values from 0 to 511, as said below
- live: int32 [128], P(('ty', 'tx')), may hold values from 1 to 16, as said below
Outputs:
- object_new: float32 [2, 8192, 4096], P(None, 'ty', 'tx')
- probe_new: float32 [2, 256, 256], replicated
Inputs may be any that keep to these rules, and one draw needn't show every extreme that they name: `offsets`: every patch lies inside the object. `live`: used slots come first in each owner's slots; some owner uses all 16.
All inputs are finite; a program needn't handle non-finite values.
Results may differ from a plain program's by a relative error of at most 0.0003.
Values sent between devices are 32-bit elements; how exact they have to be, the bound alone decides.
No kernel may reach another device: no remote copies, remote signals or barrier semaphores. Data moves between devices by JAX's collectives and lax.ppermute only.
A program may use at most 128 MiB of HBM per device.

v0:
```python
import math

import jax
import jax.numpy as jnp
from jax import lax
from jax.sharding import PartitionSpec as P

PRECISE = lax.Precision.HIGHEST


def passed_along(block, axis, distance):
    devices = range(lax.axis_size(axis))
    route = [(i - distance, i) for i in devices if i - distance in devices]
    return lax.ppermute(block, axis, route)


def dft_tables(length):
    counter = jnp.arange(length, dtype=jnp.int32)
    product = counter[:, None] * counter[None, :] % length
    angles = product.astype(jnp.float32) * (-2.0 * math.pi / length)
    factor = 1.0 / math.sqrt(length)
    return (jnp.cos(angles) * factor, jnp.sin(angles) * factor)


def apply_left(cos_part, sin_part, real_part, imag_part):

    def mult(table, values):
        return jnp.einsum("kn,snm->skm", table, values, precision=PRECISE)

    return (
        mult(cos_part, real_part) - mult(sin_part, imag_part),
        mult(cos_part, imag_part) + mult(sin_part, real_part),
    )


def apply_right(real_part, imag_part, cos_part, sin_part):

    def mult(values, table):
        return jnp.einsum("skn,nm->skm", values, table, precision=PRECISE)

    return (
        mult(real_part, cos_part) - mult(imag_part, sin_part),
        mult(real_part, sin_part) + mult(imag_part, cos_part),
    )


def transform(real_part, imag_part, cos_part, sin_part):
    left_real, left_imag = apply_left(cos_part, sin_part, real_part, imag_part)
    return apply_right(left_real, left_imag, cos_part, sin_part)


def slot_grads(patches, probe, pattern, weights, cos_part, sin_part):
    obj_real = patches[:, 0]
    obj_imag = patches[:, 1]
    probe_real = probe[0]
    probe_imag = probe[1]
    wave_real = probe_real * obj_real - probe_imag * obj_imag
    wave_imag = probe_real * obj_imag + probe_imag * obj_real
    far_real, far_imag = transform(wave_real, wave_imag, cos_part, sin_part)
    misfit = (far_real * far_real + far_imag * far_imag - pattern) * weights[:, None, None]
    back_real, back_imag = transform(misfit * far_real, misfit * far_imag, cos_part, -sin_part)
    patch_grads = jnp.stack(
        [
            probe_real * back_real + probe_imag * back_imag,
            probe_real * back_imag - probe_imag * back_real,
        ],
        axis=1,
    )
    probe_grad = jnp.stack(
        [
            jnp.sum(obj_real * back_real + obj_imag * back_imag, axis=0),
            jnp.sum(obj_real * back_imag - obj_imag * back_real, axis=0),
        ]
    )
    return (patch_grads, probe_grad)


def body(object_field, probe, measured, offsets, live):
    slots = measured.shape[0]
    side = probe.shape[1]
    tile = object_field.shape[1]
    cos_part, sin_part = dft_tables(side)
    from_right = passed_along(object_field[:, :, :side], "tx", -1)
    widened = jnp.concatenate([object_field, from_right], axis=2)
    from_below = passed_along(widened[:, :side, :], "ty", -1)
    extended = jnp.concatenate([widened, from_below], axis=1)
    live_count = live[0]
    row_offsets = offsets[:, 0]
    col_offsets = offsets[:, 1]
    anchor = jnp.zeros((), jnp.int32)

    def cut_patch(row, col):
        return lax.dynamic_slice(extended, (anchor, row, col), (2, side, side))

    def add_patch(total, patch, row, col):
        current = lax.dynamic_slice(total, (anchor, row, col), (2, side, side))
        return lax.dynamic_update_slice(total, current + patch, (anchor, row, col))

    grad_tile = jnp.zeros((2, tile + side, tile + side), jnp.float32)
    patches = jax.vmap(cut_patch)(row_offsets, col_offsets)
    weights = (jnp.arange(slots, dtype=jnp.int32) < live_count).astype(jnp.float32)
    patch_grads, probe_grad = slot_grads(patches, probe, measured, weights, cos_part, sin_part)

    def place(number, total):
        return add_patch(total, patch_grads[number], row_offsets[number], col_offsets[number])

    grad_tile = lax.fori_loop(0, slots, place, grad_tile)
    from_above = passed_along(grad_tile[:, tile:, :], "ty", 1)
    upper_part = grad_tile[:, :tile, :].at[:, :side, :].add(from_above)
    from_left = passed_along(upper_part[:, :, tile:], "tx", 1)
    own_grad = upper_part[:, :, :tile].at[:, :, :side].add(from_left)
    object_next = object_field - 0.25 * own_grad
    positions = slots * lax.axis_size("ty") * lax.axis_size("tx")
    probe_scale = 1.0 / math.sqrt(positions)
    total_grad = lax.psum(probe_grad, ("ty", "tx"))
    probe_next = probe - probe_scale * total_grad
    return (object_next, probe_next)


def solution(mesh):
    placed = (
        P(None, "ty", "tx"),
        P(),
        P(("ty", "tx"), None, None),
        P(("ty", "tx"), None),
        P(("ty", "tx")),
    )
    return jax.shard_map(
        body, mesh=mesh, in_specs=placed, out_specs=(P(None, "ty", "tx"), P()), check_vma=False
    )
```

profile of v0, /device:TPU:25, one launch (start us, length us, event | category | flops | bytes accessed | tf_op | source)
XLA Modules:
  0.0 697.6 jit_solution(14243363290889767966)
XLA Ops:
  8.5 2.9 collective-permute-start
  13.2 23.7 %collective-permute-done = f32[2,512,256]{2,1,0:T(8,128)S(1)} collective-permute-done((f32[2,512,256]{2,1,0:T(8,128)S(1)}, f32[2,512,256]{2,1,0:T(8,128)S(1)}, u32[]{:S(2)}, u32[]{:S(2)}) %collective-permute-start) | collective-permute-done | bytes 1048608 | tf_op jit(solution)/shard_map/ppermute | solution.py:14
  38.2 3.4 collective-permute-start.1
  44.1 17.6 %collective-permute-done.1 = f32[2,256,768]{2,1,0:T(8,128)} collective-permute-done((f32[2,256,768]{2,1,0:T(8,128)}, f32[2,256,768]{2,1,0:T(8,128)}, u32[]{:S(2)}, u32[]{:S(2)}) %collective-permute-start.1) | collective-permute-done | bytes 1572896 | tf_op jit(solution)/shard_map/ppermute | solution.py:14
  61.7 3.9 pad_maximum_fusion.1
  65.6 64.6 %while.17 = (s32[]{:T(128)}, f32[2,768,768]{2,1,0:T(8,128)}, s32[16,3]{0,1:T(4,128)S(1)}, f32[16,2,256,256]{3,2,0,1:T(8,128)}, s32[]{:T(128)}) while((s32[]{:T(128)}, f32[2,768,768]{2,1,0:T(8,128)}, s32[16,3]{0,1:T(4,128)S(1)}, f32[16,2,256,256]{3,2,0,1:T(8,128)}, s32[]{:T(128)}) %tuple.64), condition=%wide.while_cond.2, body=%wide.while_body.2.sunk | while | flops 2 | bytes 1050217 | solution.py:93
  66.2 3.4 bitcast_dynamic-update-slice_fusion.2
  70.3 3.4 bitcast_dynamic-update-slice_fusion.2
  74.3 3.4 bitcast_dynamic-update-slice_fusion.2
  78.4 3.4 bitcast_dynamic-update-slice_fusion.2
  82.4 3.4 bitcast_dynamic-update-slice_fusion.2
  86.4 3.4 bitcast_dynamic-update-slice_fusion.2
  90.5 3.4 bitcast_dynamic-update-slice_fusion.2
  94.5 3.4 bitcast_dynamic-update-slice_fusion.2
  98.5 3.4 bitcast_dynamic-update-slice_fusion.2
  102.6 3.4 bitcast_dynamic-update-slice_fusion.2
  106.6 3.4 bitcast_dynamic-update-slice_fusion.2
  110.6 3.4 bitcast_dynamic-update-slice_fusion.2
  114.6 3.4 bitcast_dynamic-update-slice_fusion.2
  118.7 3.4 bitcast_dynamic-update-slice_fusion.2
  122.7 3.4 bitcast_dynamic-update-slice_fusion.2
  126.7 3.4 bitcast_dynamic-update-slice_fusion.2
  130.2 11.6 %fusion.41 = f32[16,256,256]{2,1,0:T(8,128)S(1)} fusion(f32[16,2,256,256]{3,2,0,1:T(8,128)} %get-tuple-element.128, f32[256,256]{1,0:T(8,128)S(1)} %copy-done.3, f32[256,256]{1,0:T(8,128)S(1)} %get-tuple-element.162), kind=kOutput, calls=%fused_computation.53 | convolution fusion | flops 3225354240 | bytes 13107200 | tf_op jit(solution)/shard_map/kn,snm->skm/dot_general | solution.py:28
  141.8 8.2 %fusion.37 = f32[16,256,256]{2,1,0:T(8,128)S(1)} fusion(f32[16,2,256,256]{3,2,0,1:T(8,128)S(1)} %copy-done, f32[256,256]{1,0:T(8,128)S(1)} %copy-done.3, f32[256,256]{1,0:T(8,128)S(1)} %get-tuple-element.162), kind=kOutput, calls=%fused_computation.52 | convolution fusion | flops 3225354240 | bytes 13107200 | tf_op jit(solution)/shard_map/kn,snm->skm/dot_general | solution.py:28
  150.1 8.7 %convolution_add_fusion.1 = f32[16,256,256]{2,1,0:T(8,128)S(1)} fusion(f32[16,256,256]{2,1,0:T(8,128)S(1)} %fusion.37, f32[16,2,256,256]{3,2,0,1:T(8,128)S(1)} %copy-done, f32[256,256]{1,0:T(8,128)S(1)} %copy-done.3, f32[256,256]{1,0:T(8,128)S(1)} %get-tuple-element.162), kind=kOutput, calls=%fused_computation.46 | convolution fusion | flops 3226402816 | bytes 17301504 | tf_op jit(solution)/shard_map/kn,snm->skm/dot_general | solution.py:28
  158.8 8.0 %fusion.8 = f32[16,256,256]{2,1,0:T(8,128)S(1)} fusion(f32[16,256,256]{2,1,0:T(8,128)S(1)} %convolution_add_fusion.1), kind=kOutput, calls=%fused_computation.13 | convolution fusion | flops 3222208512 | bytes 8388608 | tf_op jit(solution)/shard_map/skn,nm->skm/dot_general | solution.py:39
  166.8 10.6 %fusion.10 = f32[16,256,256]{2,1,0:T(8,128)} fusion(f32[16,256,256]{2,1,0:T(8,128)S(1)} %convolution_add_fusion.1), kind=kOutput, calls=%fused_computation.15 | convolution fusion | flops 3222208512 | bytes 8388608 | tf_op jit(solution)/shard_map/skn,nm->skm/dot_general | solution.py:39
  177.4 8.3 %convolution_subtract_fusion.1 = f32[16,256,256]{2,1,0:T(8,128)S(1)} fusion(f32[16,256,256]{2,1,0:T(8,128)S(1)} %fusion.41, f32[16,2,256,256]{3,2,0,1:T(8,128)S(1)} %copy-done, f32[256,256]{1,0:T(8,128)S(1)} %copy-done.3, f32[256,256]{1,0:T(8,128)S(1)} %get-tuple-element.162), kind=kOutput, calls=%fused_computation.47 | convolution fusion | flops 3226402816 | bytes 17301504 | tf_op jit(solution)/shard_map/kn,snm->skm/dot_general | solution.py:28
  185.7 8.3 %fusion.27 = f32[16,256,256]{2,1,0:T(8,128)S(1)} fusion(f32[16,256,256]{2,1,0:T(8,128)S(1)} %fusion.8, f32[16,256,256]{2,1,0:T(8,128)S(1)} %convolution_subtract_fusion.1), kind=kOutput, calls=%fused_computation.41 | convolution fusion | flops 3223257088 | bytes 12582912 | tf_op jit(solution)/shard_map/skn,nm->skm/dot_general | solution.py:39
  194.0 13.2 %fusion.23 = (f32[16,256,256]{2,1,0:T(8,128)S(1)}, f32[16,256,256]{2,1,0:T(8,128)S(1)}) fusion(f32[16,256,256]{2,1,0:T(8,128)} %param.13, f32[16,256,256]{2,1,0:T(8,128)S(1)} %fusion.27, f32[16]{0:T(128)S(1)} %compare_convert_fusion, f32[16,256,256]{2,1,0:T(8,128)} %fusion.10, f32[16,256,256]{2,1,0:T(8,128)S(1)} %convolution_subtract_fusion.1), kind=kOutput, calls=%fused_computation.39 | convolution fusion | flops 3230597120 | bytes 25165888 | tf_op jit(solution)/shard_map/skn,nm->skm/dot_general | solution.py:39
  207.2 8.1 %fusion.58 = f32[16,256,256]{2,1,0:T(8,128)S(1)} fusion(f32[16,256,256]{2,1,0:T(8,128)S(1)} %get-tuple-element.156), kind=kOutput, calls=%fused_computation.74 | convolution fusion | flops 3222208512 | bytes 8388608 | tf_op jit(solution)/shard_map/kn,snm->skm/dot_general | solution.py:28
  215.3 7.7 %fusion.55 = f32[16,256,256]{2,1,0:T(8,128)S(1)} fusion(f32[16,256,256]{2,1,0:T(8,128)S(1)} %get-tuple-element.157), kind=kOutput, calls=%fused_computation.71 | convolution fusion | flops 3222208512 | bytes 8388608 | tf_op jit(solution)/shard_map/kn,snm->skm/dot_general | solution.py:28
  223.0 8.2 %convolution_add_fusion = f32[16,256,256]{2,1,0:T(8,128)S(1)} fusion(f32[16,256,256]{2,1,0:T(8,128)S(1)} %fusion.55, f32[16,256,256]{2,1,0:T(8,128)S(1)} %get-tuple-element.156), kind=kOutput, calls=%fused_computation.44 | convolution fusion | flops 3223322624 | bytes 12582912 | tf_op jit(solution)/shard_map/kn,snm->skm/dot_general | solution.py:28
  231.2 7.8 %fusion = f32[16,256,256]{2,1,0:T(8,128)S(1)} fusion(f32[16,256,256]{2,1,0:T(8,128)S(1)} %convolution_add_fusion), kind=kOutput, calls=%fused_computation.5 | convolution fusion | flops 3222208512 | bytes 8388608 | tf_op jit(solution)/shard_map/skn,nm->skm/dot_general | solution.py:39
  239.0 8.6 %fusion.2 = f32[16,256,256]{2,1,0:T(8,128)S(1)} fusion(f32[16,256,256]{2,1,0:T(8,128)S(1)} %convolution_add_fusion), kind=kOutput, calls=%fused_computation.7 | convolution fusion | flops 3222274048 | bytes 8388608 | tf_op jit(solution)/shard_map/skn,nm->skm/dot_general | solution.py:39
  247.6 8.2 %convolution_subtract_fusion = f32[16,256,256]{2,1,0:T(8,128)S(1)} fusion(f32[16,256,256]{2,1,0:T(8,128)S(1)} %fusion.58, f32[16,256,256]{2,1,0:T(8,128)S(1)} %get-tuple-element.157), kind=kOutput, calls=%fused_computation.45 | convolution fusion | flops 3223322624 | bytes 12582912 | tf_op jit(solution)/shard_map/kn,snm->skm/dot_general | solution.py:28
  255.8 8.3 %fusion.33 = f32[16,256,256]{2,1,0:T(8,128)S(1)} fusion(f32[16,256,256]{2,1,0:T(8,128)S(1)} %fusion, f32[16,256,256]{2,1,0:T(8,128)S(1)} %convolution_subtract_fusion), kind=kOutput, calls=%fused_computation.43 | convolution fusion | flops 3223322624 | bytes 12582912 | tf_op jit(solution)/shard_map/skn,nm->skm/dot_general | solution.py:39
  264.1 15.9 %fusion.19 = (f32[256,256]{1,0:T(8,128)}, f32[256,256]{1,0:T(8,128)}, f32[16,1,256,256]{3,2,0,1:T(8,128)}, f32[16,1,256,256]{3,2,0,1:T(8,128)}) fusion(f32[16,256,256]{2,1,0:T(8,128)S(1)} %fusion.33, f32[16,2,256,256]{3,2,0,1:T(8,128)S(1)} %copy-done, f32[256,256]{1,0:T(8,128)} %get-tuple-element.163, f32[256,256]{1,0:T(8,128)} %copy-done.2, ...), kind=kOutput, calls=%fused_computation.28 | convolution fusion | flops 3237806080 | bytes 30408704 | tf_op jit(solution)/shard_map/skn,nm->skm/dot_general | solution.py:39
  280.0 7.6 %pad_maximum_fusion = f32[16,2,256,256]{3,2,0,1:T(8,128)} fusion(f32[16,1,256,256]{3,2,0,1:T(8,128)} %get-tuple-element.160, f32[16,1,256,256]{3,2,0,1:T(8,128)} %get-tuple-element.161), kind=kLoop, calls=%fused_computation.3 | loop fusion | flops 2097152 | bytes 16777216 | tf_op jit(solution)/shard_map/stack | solution.py:62
  287.6 2.5 broadcast_in_dim.2
  290.0 212.5 %while.16 = (s32[]{:T(128)}, f32[2,768,768]{2,1,0:T(8,128)}, s32[16]{0:T(128)S(1)}, s32[16]{0:T(128)S(1)}, f32[16,2,256,256]{3,2,0,1:T(8,128)}, /*index=5*/s32[]{:T(128)}, s32[]{:T(128)}, s32[]{:T(128)}) while((s32[]{:T(128)}, f32[2,768,768]{2,1,0:T(8,128)}, s32[16]{0:T(128)S(1)}, s32[16]{0:T(128)S(1)}, f32[16,2,256,256]{3,2,0,1:T(8,128)}, ...), condition=%wide.region_1.2_spmd, body=%wide.region_0.1_spmd.sunk | while | flops 131080 | bytes 2621633 | solution.py:107
  296.6 6.8 dynamic_update_slice.8
  310.0 6.3 dynamic_update_slice.8
  322.9 6.8 dynamic_update_slice.8
  336.3 6.6 dynamic_update_slice.8
  349.4 6.4 dynamic_update_slice.8
  362.4 6.5 dynamic_update_slice.8
  375.5 6.8 dynamic_update_slice.8
  388.9 6.8 dynamic_update_slice.8
  402.3 6.8 dynamic_update_slice.8
  415.7 6.8 dynamic_update_slice.8
  429.1 6.8 dynamic_update_slice.8
  442.5 6.6 dynamic_update_slice.8
  455.7 6.8 dynamic_update_slice.8
  469.0 6.7 dynamic_update_slice.8
  482.4 6.8 dynamic_update_slice.8
  495.8 6.8 dynamic_update_slice.8
  504.0 1.9 collective-permute-start.2
  506.0 2.1 slice.94
  508.1 15.2 %collective-permute-done.2 = f32[2,256,768]{2,1,0:T(8,128)S(1)} collective-permute-done((f32[2,256,768]{2,1,0:T(8,128)S(1)}, f32[2,256,768]{2,1,0:T(8,128)S(1)}, u32[]{:S(2)}, u32[]{:S(2)}) %collective-permute-start.2) | collective-permute-done | bytes 1572896 | tf_op jit(solution)/shard_map/ppermute | solution.py:14
  526.0 2.3 collective-permute-start.3
  529.2 155.5 %all-reduce.2.cloned.1.call-done = f32[2,256,256]{2,1,0:T(8,128)} async-done(((f32[2,256,256]{2,1,0:T(8,128)}), f32[2,256,256]{2,1,0:T(8,128)}) %all-reduce.2.cloned.1.call-update) | async-done | bytes 524304 | tf_op jit(solution)/shard_map/psum | solution.py:115
  684.8 2.2 multiply_subtract_fusion.1
  688.7 1.8 multiply_subtract_fusion
  (113 shorter events, 66.2 us)
Async XLA Ops:
  7.2 677.6 %all-reduce.2.cloned.1.call-start = ((), (), s32[]{:S(2)}) async-start(), calls=%async_computation | async-start | bytes 1048576 | tf_op jit(solution)/shard_map/psum | solution.py:115
  8.5 33.8 %copy-start.6 = (s32[16,2]{0,1:T(2,128)S(1)}, s32[16,2]{0,1:T(2,128)}, u32[]{:S(2)}) copy-start(s32[16,2]{0,1:T(2,128)} %param.14) | copy-start | bytes 388
  8.5 28.3 %collective-permute-start = (f32[2,512,256]{2,1,0:T(8,128)S(1)}, f32[2,512,256]{2,1,0:T(8,128)S(1)}, u32[]{:S(2)}, u32[]{:S(2)}) collective-permute-start(f32[2,512,256]{2,1,0:T(8,128)S(1)} %slice.89), channel_id=1, source_target_pairs={{1,0},{2,1},{3,2},{4,3},{5,4},{6,5},{7,6},{9,8},{10,9},{11,10},{12... | collective-permute-start | bytes 3145736 | tf_op jit(solution)/shard_map/ppermute | solution.py:14
  38.2 23.6 %collective-permute-start.1 = (f32[2,256,768]{2,1,0:T(8,128)}, f32[2,256,768]{2,1,0:T(8,128)}, u32[]{:S(2)}, u32[]{:S(2)}) collective-permute-start(f32[2,256,768]{2,1,0:T(8,128)} %slice.115), channel_id=1, source_target_pairs={{8,0},{16,8},{24,16},{32,24},{40,32},{48,40},{56,48},{64,56},{72,6... | collective-permute-start | bytes 4718600 | tf_op jit(solution)/shard_map/ppermute | solution.py:14
  44.1 133.3 %copy-start.2 = (f32[256,256]{1,0:T(8,128)}, f32[256,256]{1,0:T(8,128)S(1)}, u32[]{:S(2)}) copy-start(f32[256,256]{1,0:T(8,128)S(1)} %get-tuple-element.162) | copy-start | bytes 786436
  65.6 64.6 %copy-start.3 = (f32[256,256]{1,0:T(8,128)S(1)}, f32[256,256]{1,0:T(8,128)}, u32[]{:S(2)}) copy-start(f32[256,256]{1,0:T(8,128)} %get-tuple-element.163) | copy-start | bytes 786436
  130.2 11.7 %copy-start = (f32[16,2,256,256]{3,2,0,1:T(8,128)S(1)}, f32[16,2,256,256]{3,2,0,1:T(8,128)}, u32[]{:S(2)}) copy-start(f32[16,2,256,256]{3,2,0,1:T(8,128)} %get-tuple-element.128) | copy-start | bytes 25165828
  504.0 19.3 %collective-permute-start.2 = (f32[2,256,768]{2,1,0:T(8,128)S(1)}, f32[2,256,768]{2,1,0:T(8,128)S(1)}, u32[]{:S(2)}, u32[]{:S(2)}) collective-permute-start(f32[2,256,768]{2,1,0:T(8,128)S(1)} %slice.96), channel_id=1, source_target_pairs={{0,8},{8,16},{16,24},{24,32},{32,40},{40,48},{48,56},{56,64},{64,7... | collective-permute-start | bytes 4718600 | tf_op jit(solution)/shard_map/ppermute | solution.py:14
  508.1 20.3 %copy-start.4 = (f32[256,256]{1,0:T(8,128)S(1)}, f32[256,256]{1,0:T(8,128)}, u32[]{:S(2)}) copy-start(f32[256,256]{1,0:T(8,128)} %get-tuple-element.134) | copy-start | bytes 786436
  508.1 20.3 %copy-start.5 = (f32[256,256]{1,0:T(8,128)S(1)}, f32[256,256]{1,0:T(8,128)}, u32[]{:S(2)}) copy-start(f32[256,256]{1,0:T(8,128)} %get-tuple-element.135) | copy-start | bytes 786436
  526.0 161.3 %collective-permute-start.3 = (f32[2,512,256]{2,1,0:T(8,128)}, f32[2,512,256]{2,1,0:T(8,128)}, u32[]{:S(2)}, u32[]{:S(2)}) collective-permute-start(f32[2,512,256]{2,1,0:T(8,128)} %slice.118), channel_id=1, source_target_pairs={{0,1},{1,2},{2,3},{3,4},{4,5},{5,6},{6,7},{8,9},{9,10},{10,11},{11... | collective-permute-start | bytes 3145736 | tf_op jit(solution)/shard_map/ppermute | solution.py:14
  684.8 4.0 copy-start.1
Sparse Core Ops, SparseCore 0:
  529.4 155.3 all-reduce.1
where the time goes:
time: 709 us; the launch traced here: 698 us
  waiting for transfers between devices  212 us (30%)
  local copies, waits for them, and re-layouts  204 us (29%)
  matrix products  150 us (21%)
  loops' own time  62.3 us (9%)
  other arithmetic  43.9 us (6%)
  between operations  15.2 us (2%)
  starting transfers between devices  10.6 us (1%)
    psum x1, waiting for transfers between devices, body(): total_grad = lax.psum(probe_grad, ('ty', 'tx'))  156 us
    dynamic_update_slice x16, local copies, waits for them, and re-layouts, add_patch(): return lax.dynamic_update_slice(total, current + patch, (anchor, row, col))  107 us
    dot_general x8, matrix products, mult(): return jnp.einsum('skn,nm->skm', values, table, precision=PRECISE)  80.6 us
    dot_general x8, matrix products, mult(): return jnp.einsum('kn,snm->skm', table, values, precision=PRECISE)  69.1 us
    gather x48, local copies, waits for them, and re-layouts  64.5 us
    another operation x1, loops' own time, body(): grad_tile = lax.fori_loop(0, slots, place, grad_tile)  62.3 us
    ppermute x4, waiting for transfers between devices, passed_along(): return lax.ppermute(block, axis, route)  56.5 us
    add x16, other arithmetic, add_patch(): return lax.dynamic_update_slice(total, current + patch, (anchor, row, col))  24.5 us
  transfers between devices with their start and end apart: 5, of which 4 were waited for; matrix products, arithmetic and copies ran while one was open for 1% of the time, Pallas kernels for 0%

commit v1 on v0

v1 whole, which is shorter than its diff:
```python
import functools
import math

import jax
import jax.numpy as jnp
import ml_dtypes
import numpy as np
from jax import lax
from jax.experimental import pallas as pl
from jax.experimental.pallas import tpu as pltpu
from jax.sharding import PartitionSpec as P

BF16 = jnp.bfloat16
F32 = jnp.float32
SIDE = 256
HALF = 128
TILE = 512
WIDE = TILE + SIDE
ROWS = 64


def split_np(table):
    high = table.astype(ml_dtypes.bfloat16)
    low = (table - high.astype(np.float64)).astype(ml_dtypes.bfloat16)
    return high, low


def dft_tables():
    k = np.arange(HALF)[:, None]
    n = np.arange(HALF)[None, :]
    forward = []
    backward = []
    for parity in range(2):
        angle = -2.0 * math.pi * ((n * (2 * k + parity)) % SIDE) / SIDE
        cos = np.cos(angle) / math.sqrt(SIDE)
        sin = np.sin(angle) / math.sqrt(SIDE)
        stacked = np.block([[cos, -sin], [sin, cos]])
        forward.extend(split_np(stacked))
        backward.extend(split_np(stacked.T))
    tables = np.stack(forward + backward).reshape(2, 2, 2, SIDE, SIDE)
    order = np.concatenate([np.arange(0, SIDE, 2), np.arange(1, SIDE, 2)])
    select = np.zeros((SIDE, SIDE), np.float32)
    select[order, np.arange(SIDE)] = 1.0
    return tables, select.astype(ml_dtypes.bfloat16)


def split(x):
    high = x.astype(BF16)
    low = (x - high.astype(F32)).astype(BF16)
    return high, low


def mm(a, b):
    return lax.dot_general(a, b, (((1,), (0,)), ((), ())), preferred_element_type=F32)


def left3(high, low, x_high, x_low):
    return mm(high, x_high) + (mm(high, x_low) + mm(low, x_high))


def right3(x_high, x_low, high, low):
    return mm(x_high, high) + (mm(x_low, high) + mm(x_high, low))


def one_slot(r, c, ext, grad, probe, pgrad, tab, sel, meas, patch, xh, xl, fa, fb):
    j = c // HALF
    s = c % HALF
    back_shift = lax.rem(HALF - s, HALF)
    lane = lax.broadcasted_iota(jnp.int32, (ROWS, HALF), 1)
    take_first = lane < HALF - s
    below_shift = lane < s

    for rc in range(0, HALF, ROWS):
        wave = []
        for t in range(2):
            cut = []
            for part in range(2):
                rolled = [
                    pltpu.roll(ext[part, j + h, pl.ds(r + t * HALF + rc, ROWS), :], back_shift, 1) for h in range(3)
                ]
                halves = [jnp.where(take_first, rolled[h], rolled[h + 1]) for h in range(2)]
                for h in range(2):
                    patch[part, h, pl.ds(t * HALF + rc, ROWS), :] = halves[h]
                cut.append(halves)
            rows = pl.ds(t * HALF + rc, ROWS)
            here = []
            for h in range(2):
                cols = pl.ds(h * HALF, HALF)
                qr = probe[0, rows, cols]
                qi = probe[1, rows, cols]
                here.append((qr * cut[0][h] - qi * cut[1][h], qr * cut[1][h] + qi * cut[0][h]))
            wave.append(here)
        for h in range(2):
            for part in range(2):
                top = wave[0][h][part]
                bottom = wave[1][h][part]
                for p, folded in enumerate((top + bottom, top - bottom)):
                    high, low = split(folded)
                    xh[p, pl.ds(part * HALF + rc, ROWS), pl.ds(h * HALF, HALF)] = high
                    xl[p, pl.ds(part * HALF + rc, ROWS), pl.ds(h * HALF, HALF)] = low

    for p in range(2):
        fa[p] = left3(tab[0, p, 0], tab[0, p, 1], xh[p], xl[p])

    for p in range(2):
        for h in range(2):
            high, low = split(meas[h, pl.ds(p, HALF, stride=2), :])
            xh[2, pl.ds(p * HALF, HALF), pl.ds(h * HALF, HALF)] = high
            xl[2, pl.ds(p * HALF, HALF), pl.ds(h * HALF, HALF)] = low
    fb[2] = mm(xh[2], sel[...]) + mm(xl[2], sel[...])

    for p in range(2):
        for rc in range(0, HALF, ROWS):
            for part in range(2):
                rows = pl.ds(part * HALF + rc, ROWS)
                near = fa[p, rows, pl.ds(0, HALF)]
                far = fa[p, rows, pl.ds(HALF, HALF)]
                for q, folded in enumerate((near + far, near - far)):
                    high, low = split(folded)
                    xh[3 + q, pl.ds(p * HALF + rc, ROWS), pl.ds(part * HALF, HALF)] = high
                    xl[3 + q, pl.ds(p * HALF + rc, ROWS), pl.ds(part * HALF, HALF)] = low

    for q in range(2):
        fb[q] = right3(xh[3 + q], xl[3 + q], tab[1, q, 0], tab[1, q, 1])

    for q in range(2):
        for rc in range(0, SIDE, ROWS):
            rows = pl.ds(rc, ROWS)
            re = fb[q, rows, pl.ds(0, HALF)]
            im = fb[q, rows, pl.ds(HALF, HALF)]
            misfit = re * re + im * im - fb[2, rows, pl.ds(q * HALF, HALF)]
            for part, value in enumerate((misfit * re, misfit * im)):
                high, low = split(value)
                xh[5 + q, rows, pl.ds(part * HALF, HALF)] = high
                xl[5 + q, rows, pl.ds(part * HALF, HALF)] = low

    for q in range(2):
        fa[2 + q] = right3(xh[5 + q], xl[5 + q], tab[0, q, 0], tab[0, q, 1])

    for p in range(2):
        for rc in range(0, HALF, ROWS):
            rows = pl.ds(p * HALF + rc, ROWS)
            for part in range(2):
                cols = pl.ds(part * HALF, HALF)
                even = fa[2, rows, cols]
                odd = fa[3, rows, cols]
                for h, value in enumerate((even + odd, even - odd)):
                    high, low = split(value)
                    xh[7 + p, pl.ds(part * HALF + rc, ROWS), pl.ds(h * HALF, HALF)] = high
                    xl[7 + p, pl.ds(part * HALF + rc, ROWS), pl.ds(h * HALF, HALF)] = low

    for p in range(2):
        fb[3 + p] = left3(tab[1, p, 0], tab[1, p, 1], xh[7 + p], xl[7 + p])

    for rc in range(0, HALF, ROWS):
        for t in range(2):
            rows = pl.ds(t * HALF + rc, ROWS)
            pieces = []
            for h in range(2):
                cols = pl.ds(h * HALF, HALF)
                er = fb[3, pl.ds(rc, ROWS), cols]
                ei = fb[3, pl.ds(HALF + rc, ROWS), cols]
                dr = fb[4, pl.ds(rc, ROWS), cols]
                di = fb[4, pl.ds(HALF + rc, ROWS), cols]
                br, bi = (er + dr, ei + di) if t == 0 else (er - dr, ei - di)
                qr = probe[0, rows, cols]
                qi = probe[1, rows, cols]
                pr = patch[0, h, rows, :]
                pi = patch[1, h, rows, :]
                pgrad[0, rows, cols] += pr * br + pi * bi
                pgrad[1, rows, cols] += pr * bi - pi * br
                pieces.append((qr * br + qi * bi, qr * bi - qi * br))
            target = pl.ds(r + t * HALF + rc, ROWS)
            for part in range(2):
                first = pltpu.roll(pieces[0][part], s, 1)
                second = pltpu.roll(pieces[1][part], s, 1)
                grad[part, j, target, :] += jnp.where(below_shift, 0.0, first)
                grad[part, j + 1, target, :] += jnp.where(below_shift, first, second)
                grad[part, j + 2, target, :] += jnp.where(below_shift, second, 0.0)


def kernel(
    count, offsets, own, right, below, corner, probe, measured, tab, sel,
    own_out, right_out, below_out, corner_out, pgrad,
    ext, grad, meas, patch, xh, xl, fa, fb, sems, msems, osems,
):
    parts = []
    for part in range(2):
        for h in range(4):
            parts.append((own.at[part, :, pl.ds(h * HALF, HALF)], ext.at[part, h, pl.ds(0, TILE), :]))
            parts.append((below.at[part, :, pl.ds(h * HALF, HALF)], ext.at[part, h, pl.ds(TILE, SIDE), :]))
        for h in range(2):
            parts.append((right.at[part, :, pl.ds(h * HALF, HALF)], ext.at[part, 4 + h, pl.ds(0, TILE), :]))
            parts.append((corner.at[part, :, pl.ds(h * HALF, HALF)], ext.at[part, 4 + h, pl.ds(TILE, SIDE), :]))
    loads = [pltpu.make_async_copy(a, b, sems.at[i]) for i, (a, b) in enumerate(parts)]
    for load in loads:
        load.start()

    def fetch(g, slot):
        return [
            pltpu.make_async_copy(measured.at[g, :, pl.ds(h * HALF, HALF)], meas.at[slot, h], msems.at[slot, h])
            for h in range(2)
        ]

    for copy in fetch(0, 0):
        copy.start()
    grad[...] = jnp.zeros_like(grad)
    pgrad[...] = jnp.zeros_like(pgrad)
    for load in loads:
        load.wait()
    total = count[0]

    def step(g, carry):
        slot = lax.rem(g, 2)

        @pl.when(g + 1 < total)
        def _():
            for copy in fetch(g + 1, 1 - slot):
                copy.start()

        for copy in fetch(g, slot):
            copy.wait()
        one_slot(
            offsets[2 * g], offsets[2 * g + 1], ext, grad, probe, pgrad, tab, sel, meas.at[slot],
            patch, xh, xl, fa, fb,
        )
        return carry

    lax.fori_loop(0, total, step, 0)

    parts = []
    for part in range(2):
        for h in range(4):
            parts.append((grad.at[part, h, pl.ds(0, TILE), :], own_out.at[part, :, pl.ds(h * HALF, HALF)]))
            parts.append((grad.at[part, h, pl.ds(TILE, SIDE), :], below_out.at[part, :, pl.ds(h * HALF, HALF)]))
        for h in range(2):
            parts.append((grad.at[part, 4 + h, pl.ds(0, TILE), :], right_out.at[part, :, pl.ds(h * HALF, HALF)]))
            parts.append((grad.at[part, 4 + h, pl.ds(TILE, SIDE), :], corner_out.at[part, :, pl.ds(h * HALF, HALF)]))
    stores = [pltpu.make_async_copy(a, b, osems.at[i]) for i, (a, b) in enumerate(parts)]
    for store in stores:
        store.start()
    for store in stores:
        store.wait()


def slots_call(count, offsets, own, right, below, corner, probe, measured):
    tables, select = dft_tables()
    any_spec = pl.BlockSpec(memory_space=pl.ANY)
    smem = pl.BlockSpec(memory_space=pltpu.SMEM)
    vmem = pl.BlockSpec(memory_space=pltpu.VMEM)
    shapes = [own.shape, right.shape, below.shape, corner.shape, probe.shape]
    return pl.pallas_call(
        kernel,
        out_shape=[jax.ShapeDtypeStruct(s, F32) for s in shapes],
        in_specs=[smem, smem, any_spec, any_spec, any_spec, any_spec, vmem, any_spec, vmem, vmem],
        out_specs=[any_spec] * 4 + [vmem],
        scratch_shapes=[
            pltpu.VMEM((2, 6, WIDE, HALF), F32),
            pltpu.VMEM((2, 6, WIDE, HALF), F32),
            pltpu.VMEM((2, 2, SIDE, HALF), F32),
            pltpu.VMEM((2, 2, SIDE, HALF), F32),
            pltpu.VMEM((9, SIDE, SIDE), BF16),
            pltpu.VMEM((9, SIDE, SIDE), BF16),
            pltpu.VMEM((4, SIDE, SIDE), F32),
            pltpu.VMEM((5, SIDE, SIDE), F32),
            pltpu.SemaphoreType.DMA((24,)),
            pltpu.SemaphoreType.DMA((2, 2)),
            pltpu.SemaphoreType.DMA((24,)),
        ],
        compiler_params=pltpu.CompilerParams(vmem_limit_bytes=40 * 1024 * 1024),
        cost_estimate=pl.CostEstimate(flops=16 * 26 * 2 * SIDE**3, bytes_accessed=20 * 2**20, transcendentals=0),
    )(count, offsets.reshape(-1), own, right, below, corner, probe, measured, jnp.asarray(tables), jnp.asarray(select))


def passed_along(block, axis, distance):
    devices = range(lax.axis_size(axis))
    route = [(i - distance, i) for i in devices if i - distance in devices]
    return lax.ppermute(block, axis, route)


def total_over_all(x):
    axes = ("ty", "tx")
    devices = lax.axis_size("ty") * lax.axis_size("tx")
    shares = lax.all_to_all(x.reshape(devices, -1), axes, 0, 0, tiled=True)
    share = jnp.sum(shares, axis=0, keepdims=True)
    copies = jnp.broadcast_to(share, shares.shape)
    return lax.all_to_all(copies, axes, 0, 0, tiled=True).reshape(x.shape)


def body(object_field, probe, measured, offsets, live):
    side = probe.shape[1]
    tile = object_field.shape[1]
    right = passed_along(object_field[:, :, :side], "tx", -1)
    below = passed_along(object_field[:, :side, :], "ty", -1)
    corner = passed_along(right[:, :side, :], "ty", -1)
    own_grad, right_grad, below_grad, corner_grad, probe_grad = slots_call(
        live, offsets, object_field, right, below, corner, probe, measured
    )
    from_corner = passed_along(corner_grad, "ty", 1)
    from_above = passed_along(below_grad, "ty", 1)
    from_left = passed_along(right_grad.at[:, :side, :].add(from_corner), "tx", 1)
    total_grad = total_over_all(probe_grad)
    own_grad = own_grad.at[:, :side, :].add(from_above).at[:, :, :side].add(from_left)
    object_next = object_field - 0.25 * own_grad
    positions = measured.shape[0] * lax.axis_size("ty") * lax.axis_size("tx")
    probe_next = probe - (1.0 / math.sqrt(positions)) * total_grad
    return (object_next, probe_next)


def solution(mesh):
    placed = (
        P(None, "ty", "tx"),
        P(),
        P(("ty", "tx"), None, None),
        P(("ty", "tx"), None),
        P(("ty", "tx")),
    )
    return jax.shard_map(
        body, mesh=mesh, in_specs=placed, out_specs=(P(None, "ty", "tx"), P()), check_vma=False
    )
```

time: 709 us -> 169 us (0.24); the launches traced: 698 us -> 167 us
  local copies, waits for them, and re-layouts: 204 us -> 16.8 us
  waiting for transfers between devices: 212 us -> 33.1 us
  matrix products: 150 us -> 0 us
  loops' own time: 62.3 us -> 0 us
  blocking collectives: 0 us -> 38 us
  other arithmetic: 43.9 us -> 10.5 us
  Pallas kernels: 0 us -> 32.9 us
  starting transfers between devices: 10.6 us -> 34.1 us
  between operations: 15.2 us -> 1.47 us
    psum x1 -> x0, waiting for transfers between devices: 156 us -> none  [body(): total_grad = lax.psum(probe_grad, ('ty', 'tx'))]
    dot_general x16 -> x0, matrix products: 150 us -> none  [the longest x8 80.6 us: mult(): return jnp.einsum('skn,nm->skm', values, table, precision=PRECISE)]
    dynamic_update_slice x16 -> x0, local copies, waits for them, and re-layouts: 107 us -> none  [add_patch(): return lax.dynamic_update_slice(total, current + patch, (anchor, row, col))]
    gather x48 -> x0, local copies, waits for them, and re-layouts: 64.5 us -> none
    another operation x2 -> x0, loops' own time: 62.3 us -> none  [the longest x1 62.3 us: body(): grad_tile = lax.fori_loop(0, slots, place, grad_tile)]
    all_to_all x0 -> x1, blocking collectives: none -> 38 us  [total_over_all(): return lax.all_to_all(copies, axes, 0, 0, tiled=True).reshape(x.shape)]
    pallas_call x0 -> x1, Pallas kernels: none -> 32.9 us  [slots_call(): pl.pallas_call(kernel, out_shape=[jax.ShapeDtypeStruct(s, F32) for s in s...]
    ppermute x4 -> x6, waiting for transfers between devices: 56.5 us -> 30.9 us  [passed_along(): return lax.ppermute(block, axis, route)]
  transfers between devices with their start and end apart: 5 -> 7, of which waited for: 4 -> 4; matrix products, arithmetic and copies ran while one was open for 1% -> 6% of each run, Pallas kernels for 0% -> 0%
where the time goes in v1:
time: 169 us; the launch traced here: 167 us
  blocking collectives  38 us (22%)
  starting transfers between devices  34.1 us (20%)
  waiting for transfers between devices  33.1 us (20%)
  Pallas kernels  32.9 us (19%)
  local copies, waits for them, and re-layouts  16.8 us (10%)
  other arithmetic  10.5 us (6%)
    all_to_all x1, blocking collectives, total_over_all(): return lax.all_to_all(copies, axes, 0, 0, tiled=True).reshape(x.shape)  38 us
    pallas_call x1, Pallas kernels, slots_call(): pl.pallas_call(kernel, out_shape=[jax.ShapeDtypeStruct(s, F32) for s in s...  32.9 us
    ppermute x6, waiting for transfers between devices, passed_along(): return lax.ppermute(block, axis, route)  30.9 us
    ppermute x6, starting transfers between devices, passed_along(): return lax.ppermute(block, axis, route)  18.7 us
    all_to_all x1, starting transfers between devices, total_over_all(): shares = lax.all_to_all(x.reshape(devices, -1), axes, 0, 0, tiled=True)  15.4 us
    unnamed x31, local copies, waits for them, and re-layouts  11.4 us
  transfers between devices with their start and end apart: 7, of which 4 were waited for; matrix products, arithmetic and copies ran while one was open for 6% of the time, Pallas kernels for 0%

profile of v1, /device:TPU:25, one launch (start us, length us, event | category | flops | bytes accessed | tf_op | source)
XLA Modules:
  0.0 166.8 jit_solution(17274188334390673329)
XLA Ops:
  0.6 0.0 copy-start
  0.6 1.4 slice.81
  2.1 0.0 copy-start.14
  2.1 0.0 copy-start.3
  2.1 0.0 copy-start.13
  2.1 3.0 %collective-permute-start = (f32[2,512,256]{2,1,0:T(8,128)S(1)}, f32[2,512,256]{2,1,0:T(8,128)S(1)}, u32[]{:S(2)}, u32[]{:S(2)}) collective-permute-start(f32[2,512,256]{2,1,0:T(8,128)S(1)} %slice.81), channel_id=1, source_target_pairs={{1,0},{2,1},{3,2},{4,3},{5,4},{6,5},{7,6},{9,8},{10,9},{11,10},{12... | collective-permute-start | bytes 3145736 | tf_op jit(solution)/shard_map/ppermute | solution.py:278
  5.1 0.0 copy-done
  5.1 1.1 slice.82
  6.2 2.9 %collective-permute-start.1 = (f32[2,256,512]{2,1,0:T(8,128)}, f32[2,256,512]{2,1,0:T(8,128)S(1)}, u32[]{:S(2)}, u32[]{:S(2)}) collective-permute-start(f32[2,256,512]{2,1,0:T(8,128)} %slice.82), channel_id=1, source_target_pairs={{8,0},{16,8},{24,16},{32,24},{40,32},{48,40},{56,48},{64,56},{72,6... | collective-permute-start | bytes 3145736 | tf_op jit(solution)/shard_map/ppermute | solution.py:278
  9.0 21.6 %collective-permute-done.right = f32[2,512,256]{2,1,0:T(8,128)S(1)} collective-permute-done((f32[2,512,256]{2,1,0:T(8,128)S(1)}, f32[2,512,256]{2,1,0:T(8,128)S(1)}, u32[]{:S(2)}, u32[]{:S(2)}) %collective-permute-start) | collective-permute-done | bytes 1048608 | tf_op jit(solution)/shard_map/ppermute | solution.py:278
  30.7 0.0 copy-start.5
  30.7 1.0 copy-done.5
  31.6 3.5 %collective-permute-start.2 = (f32[2,256,256]{2,1,0:T(8,128)S(1)}, f32[2,256,256]{2,1,0:T(8,128)S(1)}, u32[]{:S(2)}, u32[]{:S(2)}) collective-permute-start(f32[2,256,256]{2,1,0:T(8,128)S(1)} %slice.87), channel_id=1, source_target_pairs={{8,0},{16,8},{24,16},{32,24},{40,32},{48,40},{56,48},{64,56},{72,6... | collective-permute-start | bytes 1572872 | tf_op jit(solution)/shard_map/ppermute | solution.py:278
  35.8 0.0 copy-done.14
  35.8 0.1 copy.11
  35.9 0.1 reshape.110.offsets
  36.0 4.7 %collective-permute-done.1.below = f32[2,256,512]{2,1,0:T(8,128)S(1)} collective-permute-done((f32[2,256,512]{2,1,0:T(8,128)}, f32[2,256,512]{2,1,0:T(8,128)S(1)}, u32[]{:S(2)}, u32[]{:S(2)}) %collective-permute-start.1) | collective-permute-done | bytes 1048608 | tf_op jit(solution)/shard_map/ppermute | solution.py:278
  40.7 0.0 copy-start.8
  40.7 1.0 copy-done.8
  41.7 4.6 %collective-permute-done.2.corner = f32[2,256,256]{2,1,0:T(8,128)S(1)} collective-permute-done((f32[2,256,256]{2,1,0:T(8,128)S(1)}, f32[2,256,256]{2,1,0:T(8,128)S(1)}, u32[]{:S(2)}, u32[]{:S(2)}) %collective-permute-start.2) | collective-permute-done | bytes 524320 | tf_op jit(solution)/shard_map/ppermute | solution.py:278
  46.3 0.0 copy-start.10
  46.3 0.8 copy-done.10
  47.1 0.0 copy-done.3
  47.1 0.0 copy-done.13
  47.1 0.0 copy-start.1
  47.1 1.6 copy-done.1
  48.7 0.0 copy-start.6
  48.7 1.2 copy-done.6
  49.9 0.0 copy-start.9
  49.9 1.2 copy-done.9
  51.1 0.0 copy-start.11
  51.1 1.0 copy-done.11
  52.2 0.0 copy-start.12
  52.2 1.2 copy-done.12
  53.4 32.9 %shard_map.86 = (f32[2,512,512]{2,1,0:T(8,128)S(1)}, f32[2,512,256]{2,1,0:T(8,128)S(1)}, f32[2,256,512]{2,1,0:T(8,128)S(1)}, f32[2,256,256]{2,1,0:T(8,128)}, f32[2,256,256]{2,1,0:T(8,128)S(1)}) custom-call(s32[1]{0:T(128)S(6)} %copy.16.count, s32[32]{0:T(128)S(1)} %reshape.110.offsets, f32[2,512,512]{2,1,0:T(8,128)S(1)} %copy-done.1, ...), custom_call_target="tpu_custom_call" | custom-call | flops 13958643712 | bytes 20971520 | tf_op jit(solution)/shard_map/pallas_call | solution.py:252
  86.4 0.0 copy-start.4
  86.4 1.0 copy-done.4
  87.4 0.0 copy-start.7
  87.4 1.0 copy-done.7
  88.3 1.9 %collective-permute-start.4 = (f32[2,256,256]{2,1,0:T(8,128)}, f32[2,256,256]{2,1,0:T(8,128)}, u32[]{:S(2)}, u32[]{:S(2)}) collective-permute-start(f32[2,256,256]{2,1,0:T(8,128)} %get-tuple-element.46), channel_id=1, source_target_pairs={{0,8},{8,16},{16,24},{24,32},{32,40},{40,48},{48,56},{56,64},{64,7... | collective-permute-start | bytes 1572872 | tf_op jit(solution)/shard_map/ppermute | solution.py:278
  90.2 1.3 all_to_all.13
  91.6 15.4 %all-to-all-start = ((f32[128,1,1024]{2,1,0:T(1,128)}), f32[128,1,1024]{2,1,0:T(1,128)S(1)}, u32[]{:S(2)}, u32[]{:S(2)}) async-start(f32[128,1,1024]{2,1,0:T(1,128)} %all_to_all.13), calls=%async_computation | async-start | bytes 1048576 | tf_op jit(solution)/shard_map/all_to_all | solution.py:284
  107.0 3.8 %collective-permute-start.3 = (f32[2,256,512]{2,1,0:T(8,128)}, f32[2,256,512]{2,1,0:T(8,128)}, u32[]{:S(2)}, u32[]{:S(2)}) collective-permute-start(f32[2,256,512]{2,1,0:T(8,128)} %copy-done.7), channel_id=1, source_target_pairs={{0,8},{8,16},{16,24},{24,32},{32,40},{40,48},{48,56},{56,64},{64,7... | collective-permute-start | bytes 3145736 | tf_op jit(solution)/shard_map/ppermute | solution.py:278
  110.9 0.0 collective-permute-done.4
  110.9 2.1 %add_dynamic-update-slice_fusion.1 = f32[2,512,256]{2,1,0:T(8,128)} fusion(f32[2,512,256]{2,1,0:T(8,128)} %copy-done.4, f32[2,256,256]{2,1,0:T(8,128)} %collective-permute-done.4), kind=kLoop, calls=%fused_computation.5 | loop fusion | flops 131072 | bytes 1572864 | tf_op jit(solution)/shard_map/scatter-add | solution.py:301
  113.0 3.6 %collective-permute-start.5 = (f32[2,512,256]{2,1,0:T(8,128)}, f32[2,512,256]{2,1,0:T(8,128)}, u32[]{:S(2)}, u32[]{:S(2)}) collective-permute-start(f32[2,512,256]{2,1,0:T(8,128)} %add_dynamic-update-slice_fusion.1), channel_id=1, source_target_pairs={{0,1},{1,2},{2,3},{3,4},{4,5},{5,6},{6,7},{8,9},{9,10},{10,11},{11... | collective-permute-start | bytes 3145736 | tf_op jit(solution)/shard_map/ppermute | solution.py:278
  116.5 2.1 %all-to-all-done = f32[128,1,1024]{2,1,0:T(1,128)S(1)} async-done(((f32[128,1,1024]{2,1,0:T(1,128)}), f32[128,1,1024]{2,1,0:T(1,128)S(1)}, u32[]{:S(2)}, u32[]{:S(2)}) %all-to-all-start) | async-done | bytes 524320 | tf_op jit(solution)/shard_map/all_to_all | solution.py:284
  118.7 0.3 reduce_sum.9
  119.0 0.3 broadcast_in_dim.2
  119.3 38.0 %all_to_all.16 = f32[128,1,1024]{2,1,0:T(1,128)S(1)} all-to-all(f32[128,1,1024]{2,1,0:T(1,128)S(1)} %broadcast_in_dim.2), channel_id=1, replica_groups=mesh['ty'=16,'tx'=8] {'ty','tx'}, dimensions={0} | all-to-all | bytes 1048576 | tf_op jit(solution)/shard_map/all_to_all | solution.py:287
  157.3 2.3 %multiply_reduce_fusion = f32[128,1024]{1,0:T(8,128)} fusion(f32[128,1,1024]{2,1,0:T(1,128)S(1)} %all_to_all.16), kind=kLoop, calls=%fused_computation.4 | loop fusion | flops 131072 | bytes 1048576 | tf_op jit(solution)/shard_map/mul | solution.py:306
  159.6 1.2 mul.19
  160.8 0.9 sub.7
  161.6 0.0 collective-permute-done.3
  161.6 1.5 add_dynamic-update-slice_fusion
  163.1 0.0 copy-start.2
  163.1 0.0 collective-permute-done.5
  163.2 1.6 fusion
  164.8 0.2 copy-done.2
  165.0 1.8 %multiply_subtract_fusion = f32[2,512,512]{2,1,0:T(8,128)} fusion(f32[2,512,512]{2,1,0:T(8,128)S(1)} %copy-done.2, f32[2,512,512]{2,1,0:T(8,128)S(1)} %fusion), kind=kLoop, calls=%fused_computation | loop fusion | flops 1048576 | bytes 6291456 | tf_op jit(solution)/shard_map/sub | solution.py:304
  (1 shorter events, 0.0 us)
Async XLA Ops:
  0.6 4.5 %copy-start = (f32[2,512,512]{2,1,0:T(8,128)S(1)}, f32[2,512,512]{2,1,0:T(8,128)}, u32[]{:S(2)}) copy-start(f32[2,512,512]{2,1,0:T(8,128)} %own.1) | copy-start | bytes 6291460
  2.1 33.7 %copy-start.14 = (s32[16,2]{0,1:T(2,128)S(1)}, s32[16,2]{0,1:T(2,128)}, u32[]{:S(2)}) copy-start(s32[16,2]{0,1:T(2,128)} %param.16) | copy-start | bytes 388
  2.1 45.0 %copy-start.3 = (f32[2,256,256]{2,1,0:T(8,128)S(1)}, f32[2,256,256]{2,1,0:T(8,128)}, u32[]{:S(2)}) copy-start(f32[2,256,256]{2,1,0:T(8,128)} %probe.1) | copy-start | bytes 1572868
  2.1 45.0 %copy-start.13 = (bf16[256,256]{1,0:T(8,128)(2,1)S(1)}, bf16[256,256]{1,0:T(8,128)(2,1)}, u32[]{:S(2)}) copy-start(bf16[256,256]{1,0:T(8,128)(2,1)} %constant.83.clone.sel) | copy-start | bytes 393220
  2.1 28.5 %collective-permute-start = (f32[2,512,256]{2,1,0:T(8,128)S(1)}, f32[2,512,256]{2,1,0:T(8,128)S(1)}, u32[]{:S(2)}, u32[]{:S(2)}) collective-permute-start(f32[2,512,256]{2,1,0:T(8,128)S(1)} %slice.81), channel_id=1, source_target_pairs={{1,0},{2,1},{3,2},{4,3},{5,4},{6,5},{7,6},{9,8},{10,9},{11,10},{12... | collective-permute-start | bytes 3145736 | tf_op jit(solution)/shard_map/ppermute | solution.py:278
  6.2 34.5 %collective-permute-start.1 = (f32[2,256,512]{2,1,0:T(8,128)}, f32[2,256,512]{2,1,0:T(8,128)S(1)}, u32[]{:S(2)}, u32[]{:S(2)}) collective-permute-start(f32[2,256,512]{2,1,0:T(8,128)} %slice.82), channel_id=1, source_target_pairs={{8,0},{16,8},{24,16},{32,24},{40,32},{48,40},{56,48},{64,56},{72,6... | collective-permute-start | bytes 3145736 | tf_op jit(solution)/shard_map/ppermute | solution.py:278
  30.7 1.0 copy-start.5
  31.6 14.7 %collective-permute-start.2 = (f32[2,256,256]{2,1,0:T(8,128)S(1)}, f32[2,256,256]{2,1,0:T(8,128)S(1)}, u32[]{:S(2)}, u32[]{:S(2)}) collective-permute-start(f32[2,256,256]{2,1,0:T(8,128)S(1)} %slice.87), channel_id=1, source_target_pairs={{8,0},{16,8},{24,16},{32,24},{40,32},{48,40},{56,48},{64,56},{72,6... | collective-permute-start | bytes 1572872 | tf_op jit(solution)/shard_map/ppermute | solution.py:278
  40.7 1.0 copy-start.8
  46.3 0.8 copy-start.10
  47.1 1.6 copy-start.1
  48.7 1.2 copy-start.6
  49.9 1.2 copy-start.9
  51.1 1.0 copy-start.11
  52.2 1.2 copy-start.12
  86.4 1.0 copy-start.4
  87.4 1.0 copy-start.7
  88.3 22.5 %collective-permute-start.4 = (f32[2,256,256]{2,1,0:T(8,128)}, f32[2,256,256]{2,1,0:T(8,128)}, u32[]{:S(2)}, u32[]{:S(2)}) collective-permute-start(f32[2,256,256]{2,1,0:T(8,128)} %get-tuple-element.46), channel_id=1, source_target_pairs={{0,8},{8,16},{16,24},{24,32},{32,40},{40,48},{48,56},{56,64},{64,7... | collective-permute-start | bytes 1572872 | tf_op jit(solution)/shard_map/ppermute | solution.py:278
  91.6 27.1 %all-to-all-start = ((f32[128,1,1024]{2,1,0:T(1,128)}), f32[128,1,1024]{2,1,0:T(1,128)S(1)}, u32[]{:S(2)}, u32[]{:S(2)}) async-start(f32[128,1,1024]{2,1,0:T(1,128)} %all_to_all.13), calls=%async_computation | async-start | bytes 1048576 | tf_op jit(solution)/shard_map/all_to_all | solution.py:284
  107.0 54.6 %collective-permute-start.3 = (f32[2,256,512]{2,1,0:T(8,128)}, f32[2,256,512]{2,1,0:T(8,128)}, u32[]{:S(2)}, u32[]{:S(2)}) collective-permute-start(f32[2,256,512]{2,1,0:T(8,128)} %copy-done.7), channel_id=1, source_target_pairs={{0,8},{8,16},{16,24},{24,32},{32,40},{40,48},{48,56},{56,64},{64,7... | collective-permute-start | bytes 3145736 | tf_op jit(solution)/shard_map/ppermute | solution.py:278
  113.0 50.2 %collective-permute-start.5 = (f32[2,512,256]{2,1,0:T(8,128)}, f32[2,512,256]{2,1,0:T(8,128)}, u32[]{:S(2)}, u32[]{:S(2)}) collective-permute-start(f32[2,512,256]{2,1,0:T(8,128)} %add_dynamic-update-slice_fusion.1), channel_id=1, source_target_pairs={{0,1},{1,2},{2,3},{3,4},{4,5},{5,6},{6,7},{8,9},{9,10},{10,11},{11... | collective-permute-start | bytes 3145736 | tf_op jit(solution)/shard_map/ppermute | solution.py:278
  163.1 1.9 %copy-start.2 = (f32[2,512,512]{2,1,0:T(8,128)S(1)}, f32[2,512,512]{2,1,0:T(8,128)}, u32[]{:S(2)}) copy-start(f32[2,512,512]{2,1,0:T(8,128)} %own.1) | copy-start | bytes 6291460

commit v2 on v1

v2 whole, which is shorter than its diff:
```python
import functools
import math

import jax
import jax.numpy as jnp
import ml_dtypes
import numpy as np
from jax import lax
from jax.experimental import pallas as pl
from jax.experimental.pallas import tpu as pltpu
from jax.sharding import PartitionSpec as P

BF16 = jnp.bfloat16
F32 = jnp.float32
SIDE = 256
HALF = 128
TILE = 512
WIDE = TILE + SIDE
ROWS = 64


def split_np(table):
    high = table.astype(ml_dtypes.bfloat16)
    low = (table - high.astype(np.float64)).astype(ml_dtypes.bfloat16)
    return high, low


def dft_tables():
    k = np.arange(HALF)[:, None]
    n = np.arange(HALF)[None, :]
    forward = []
    backward = []
    for parity in range(2):
        angle = -2.0 * math.pi * ((n * (2 * k + parity)) % SIDE) / SIDE
        cos = np.cos(angle) / math.sqrt(SIDE)
        sin = np.sin(angle) / math.sqrt(SIDE)
        stacked = np.block([[cos, -sin], [sin, cos]])
        forward.extend(split_np(stacked))
        backward.extend(split_np(stacked.T))
    tables = np.stack(forward + backward).reshape(2, 2, 2, SIDE, SIDE)
    order = np.concatenate([np.arange(0, SIDE, 2), np.arange(1, SIDE, 2)])
    select = np.zeros((SIDE, SIDE), np.float32)
    select[order, np.arange(SIDE)] = 1.0
    return tables, select.astype(ml_dtypes.bfloat16)


def split(x):
    high = x.astype(BF16)
    low = (x - high.astype(F32)).astype(BF16)
    return high, low


def mm(a, b):
    return lax.dot_general(a, b, (((1,), (0,)), ((), ())), preferred_element_type=F32)


def left3(high, low, x_high, x_low):
    return mm(high, x_high) + (mm(high, x_low) + mm(low, x_high))


def right3(x_high, x_low, high, low):
    return mm(x_high, high) + (mm(x_low, high) + mm(x_high, low))


def cut_steps(r, c, ext, probe, patch, xh, xl):
    j = c // HALF
    back_shift = lax.rem(HALF - c % HALF, HALF)
    lane = lax.broadcasted_iota(jnp.int32, (ROWS, HALF), 1)
    take_first = lane < HALF - c % HALF

    def chunk(rc):
        wave = []
        for t in range(2):
            cut = []
            rows = pl.ds(t * HALF + rc, ROWS)
            for part in range(2):
                rolled = [
                    pltpu.roll(ext[part, j + h, pl.ds(r + t * HALF + rc, ROWS), :], back_shift, 1) for h in range(3)
                ]
                halves = [jnp.where(take_first, rolled[h], rolled[h + 1]) for h in range(2)]
                for h in range(2):
                    patch[part, h, rows, :] = halves[h]
                cut.append(halves)
            here = []
            for h in range(2):
                cols = pl.ds(h * HALF, HALF)
                qr = probe[0, rows, cols]
                qi = probe[1, rows, cols]
                here.append((qr * cut[0][h] - qi * cut[1][h], qr * cut[1][h] + qi * cut[0][h]))
            wave.append(here)
        for h in range(2):
            for part in range(2):
                top = wave[0][h][part]
                bottom = wave[1][h][part]
                for p, folded in enumerate((top + bottom, top - bottom)):
                    high, low = split(folded)
                    xh[p, pl.ds(part * HALF + rc, ROWS), pl.ds(h * HALF, HALF)] = high
                    xl[p, pl.ds(part * HALF + rc, ROWS), pl.ds(h * HALF, HALF)] = low

    return [functools.partial(chunk, rc) for rc in range(0, HALF, ROWS)]


def transform_steps(meas, tab, sel, xh, xl, fa, fb):
    first, middle = [], []

    def left(out, k, table, p, source):
        out[k] = left3(tab[table, p, 0], tab[table, p, 1], xh[source], xl[source])

    def right(out, k, table, q, source):
        out[k] = right3(xh[source], xl[source], tab[table, q, 0], tab[table, q, 1])

    def sort_measured(p, h):
        high, low = split(meas[h, pl.ds(p, HALF, stride=2), :])
        xh[2, pl.ds(p * HALF, HALF), pl.ds(h * HALF, HALF)] = high
        xl[2, pl.ds(p * HALF, HALF), pl.ds(h * HALF, HALF)] = low

    def select():
        fb[2] = mm(xh[2], sel[...]) + mm(xl[2], sel[...])

    def fold_cols(p, rc):
        for part in range(2):
            rows = pl.ds(part * HALF + rc, ROWS)
            near = fa[p, rows, pl.ds(0, HALF)]
            far = fa[p, rows, pl.ds(HALF, HALF)]
            for q, folded in enumerate((near + far, near - far)):
                high, low = split(folded)
                xh[3 + q, pl.ds(p * HALF + rc, ROWS), pl.ds(part * HALF, HALF)] = high
                xl[3 + q, pl.ds(p * HALF + rc, ROWS), pl.ds(part * HALF, HALF)] = low

    def misfit(q, rc):
        rows = pl.ds(rc, ROWS)
        re = fb[q, rows, pl.ds(0, HALF)]
        im = fb[q, rows, pl.ds(HALF, HALF)]
        miss = re * re + im * im - fb[2, rows, pl.ds(q * HALF, HALF)]
        for part, value in enumerate((miss * re, miss * im)):
            high, low = split(value)
            xh[5 + q, rows, pl.ds(part * HALF, HALF)] = high
            xl[5 + q, rows, pl.ds(part * HALF, HALF)] = low

    def unfold_cols(p, rc):
        rows = pl.ds(p * HALF + rc, ROWS)
        for part in range(2):
            cols = pl.ds(part * HALF, HALF)
            even = fa[2, rows, cols]
            odd = fa[3, rows, cols]
            for h, value in enumerate((even + odd, even - odd)):
                high, low = split(value)
                xh[7 + p, pl.ds(part * HALF + rc, ROWS), pl.ds(h * HALF, HALF)] = high
                xl[7 + p, pl.ds(part * HALF + rc, ROWS), pl.ds(h * HALF, HALF)] = low

    part = functools.partial
    first = [part(sort_measured, p, h) for p in range(2) for h in range(2)]
    first = [part(left, fa, 0, 0, 0, 0)] + first[:2] + [part(left, fa, 1, 0, 1, 1)] + first[2:] + [select]
    first += [part(fold_cols, p, rc) for p in range(2) for rc in range(0, HALF, ROWS)]
    middle = [part(right, fb, 0, 1, 0, 3), part(right, fb, 1, 1, 1, 4)]
    middle += [part(misfit, q, rc) for q in range(2) for rc in range(0, SIDE, ROWS)]
    middle += [part(right, fa, 2, 0, 0, 5), part(right, fa, 3, 0, 1, 6)]
    middle += [part(unfold_cols, p, rc) for p in range(2) for rc in range(0, HALF, ROWS)]
    middle += [part(left, fb, 3, 1, 0, 7), part(left, fb, 4, 1, 1, 8)]
    return first, middle


def grad_steps(r, c, grad, probe, pgrad, patch, fb):
    j = c // HALF
    s = c % HALF
    lane = lax.broadcasted_iota(jnp.int32, (ROWS, HALF), 1)
    below_shift = lane < s

    def chunk(rc, t):
        rows = pl.ds(t * HALF + rc, ROWS)
        pieces = []
        for h in range(2):
            cols = pl.ds(h * HALF, HALF)
            er = fb[3, pl.ds(rc, ROWS), cols]
            ei = fb[3, pl.ds(HALF + rc, ROWS), cols]
            dr = fb[4, pl.ds(rc, ROWS), cols]
            di = fb[4, pl.ds(HALF + rc, ROWS), cols]
            br, bi = (er + dr, ei + di) if t == 0 else (er - dr, ei - di)
            qr = probe[0, rows, cols]
            qi = probe[1, rows, cols]
            pr = patch[0, h, rows, :]
            pi = patch[1, h, rows, :]
            pgrad[0, h, rows, :] += pr * br + pi * bi
            pgrad[1, h, rows, :] += pr * bi - pi * br
            pieces.append((qr * br + qi * bi, qr * bi - qi * br))
        target = pl.ds(r + t * HALF + rc, ROWS)
        for part in range(2):
            first = pltpu.roll(pieces[0][part], s, 1)
            second = pltpu.roll(pieces[1][part], s, 1)
            grad[part, j, target, :] += jnp.where(below_shift, 0.0, first)
            grad[part, j + 1, target, :] += jnp.where(below_shift, first, second)
            grad[part, j + 2, target, :] += jnp.where(below_shift, second, 0.0)

    return [functools.partial(chunk, rc, t) for rc in range(0, HALF, ROWS) for t in range(2)]


def interleaved(main, side):
    done = 0
    for i, step in enumerate(main):
        step()
        upto = (i + 1) * len(side) // len(main)
        for other in side[done:upto]:
            other()
        done = upto


def slots_kernel(plan, *refs):
    live, offsets, probe_in, pgrad_in, tab_in, sel_in, measured = refs[:7]
    n_in, n_out = len(plan["in"]), len(plan["out"])
    blocks = refs[7:7 + n_in]
    outs = refs[7 + n_in:7 + n_in + n_out]
    pgrad_out = refs[7 + n_in + n_out]
    pgrad, probe, tab, sel, ext, grad, meas, patch, xh, xl, fa, fb, order, sems, msems = refs[8 + n_in + n_out:]
    slots = measured.shape[0]

    early, late = [(probe_in, probe)], [(tab_in, tab), (sel_in, sel)]
    if plan["keep"]:
        pgrad[...] = jnp.zeros_like(pgrad)
    else:
        late.append((pgrad_in, pgrad))
    for (kind, panel, row, panels), block in zip(plan["in"], blocks):
        if kind == "grad":
            late.append((block, grad.at[:, pl.ds(panel, panels), pl.ds(row, block.shape[2]), :]))
            continue
        for part in range(2):
            first = block.shape[2] // HALF - panels
            for h in range(panels):
                early.append((
                    block.at[part, :, pl.ds((first + h) * HALF, HALF)],
                    ext.at[part, panel + h, pl.ds(row, block.shape[1]), :],
                ))
    loads = [pltpu.make_async_copy(*pair, sems.at[i]) for i, pair in enumerate(early + late)]
    for load in loads:
        load.start()
    for panel, panels, row, rows in plan["zero"]:
        grad[:, pl.ds(panel, panels), pl.ds(row, rows), :] = jnp.zeros((2, panels, rows, HALF), F32)

    def collect(g, n):
        order[n] = g
        r, c = offsets[0, g], offsets[1, g]
        inside = (r <= TILE - SIDE) & (c <= TILE - SIDE)
        used = (g < live[0]) & (inside if plan["keep"] else ~inside)
        return n + used.astype(jnp.int32)

    total = lax.fori_loop(0, slots, collect, jnp.int32(0))

    def fetch(n):
        slot = lax.rem(n, 2)
        return [
            pltpu.make_async_copy(measured.at[order[n], :, pl.ds(h * HALF, HALF)], meas.at[slot, h], msems.at[slot, h])
            for h in range(2)
        ]

    @pl.when(total > 0)
    def _():
        for copy in fetch(0):
            copy.start()

    for load in loads[:len(early)]:
        load.wait()

    def place(n):
        g = order[n]
        return offsets[0, g], offsets[1, g]

    @pl.when(total > 0)
    def _():
        fb[pl.ds(3, 2)] = jnp.zeros((2, SIDE, SIDE), F32)
        patch[2] = jnp.zeros((2, 2, SIDE, HALF), F32)
        r, c = place(0)
        for run in cut_steps(r, c, ext, probe, patch.at[0], xh, xl):
            run()
        for load in loads[len(early):]:
            load.wait()

        def step(n, carry):
            @pl.when(n + 1 < total)
            def _():
                for copy in fetch(n + 1):
                    copy.start()

            for copy in fetch(n):
                copy.wait()
            first, middle = transform_steps(meas.at[lax.rem(n, 2)], tab, sel, xh, xl, fa, fb)
            r, c = place(jnp.maximum(n - 1, 0))
            interleaved(
                first, grad_steps(r, c, grad, probe, pgrad, patch.at[lax.rem(n + 2, 3)], fb)
            )
            r, c = place(jnp.minimum(n + 1, total - 1))
            interleaved(middle, cut_steps(r, c, ext, probe, patch.at[lax.rem(n + 1, 3)], xh, xl))
            return carry

        lax.fori_loop(0, total, step, 0)
        r, c = place(total - 1)
        for run in grad_steps(r, c, grad, probe, pgrad, patch.at[lax.rem(total + 2, 3)], fb):
            run()

    @pl.when(total == 0)
    def _():
        for load in loads[len(early):]:
            load.wait()

    stores = [pltpu.make_async_copy(pgrad, pgrad_out, sems.at[0])]
    for (kind, panel, row, panels), out in zip(plan["out"], outs):
        if kind == "grad":
            pairs = [(grad.at[:, pl.ds(panel, panels), pl.ds(row, out.shape[2]), :], out)]
        else:
            pairs = []
            for part in range(2):
                first = out.shape[2] // HALF - panels
                for h in range(panels):
                    pairs.append((
                        grad.at[part, panel + h, pl.ds(row, out.shape[1]), :],
                        out.at[part, :, pl.ds((first + h) * HALF, HALF)],
                    ))
        for source, target in pairs:
            stores.append(pltpu.make_async_copy(source, target, sems.at[len(stores)]))
    for store in stores:
        store.start()
    for store in stores:
        store.wait()


PLAN_OWN = {
    "panels": 5, "keep": True,
    "in": [("ext", 0, 0, 4)],
    "zero": [(0, 4, 0, TILE)],
    "out": [("grad", 0, 0, 4)], "shapes": [(2, 4, TILE, HALF)],
}
PLAN_OUTER = {
    "panels": 6, "keep": False,
    "in": [("ext", 0, 0, 4), ("ext", 0, TILE, 4), ("ext", 4, 0, 2), ("ext", 4, TILE, 2), ("grad", 0, 0, 4)],
    "zero": [(0, 4, TILE, SIDE), (4, 2, 0, WIDE)],
    "out": [
        ("array", 4, TILE, 2), ("array", 4, 0, 2), ("array", 0, TILE, 2), ("array", 2, TILE, 2), ("array", 0, 0, 4),
    ],
    "shapes": [(2, SIDE, SIDE), (2, TILE, SIDE), (2, SIDE, SIDE), (2, SIDE, SIDE), (2, TILE, TILE)],
}


def slots_call(plan, live, offsets, probe, probe_grad, measured, blocks):
    tables, select = dft_tables()
    any_spec = pl.BlockSpec(memory_space=pl.ANY)
    smem = pl.BlockSpec(memory_space=pltpu.SMEM)
    shapes = plan["shapes"] + [(2, 2, SIDE, HALF)]
    rows, panels = WIDE, plan["panels"]
    return pl.pallas_call(
        functools.partial(slots_kernel, plan),
        out_shape=[jax.ShapeDtypeStruct(s, F32) for s in shapes],
        in_specs=[smem, smem] + [any_spec] * (5 + len(blocks)),
        out_specs=[any_spec] * len(shapes),
        scratch_shapes=[
            pltpu.VMEM((2, 2, SIDE, HALF), F32),
            pltpu.VMEM(probe.shape, F32),
            pltpu.VMEM(tables.shape, BF16),
            pltpu.VMEM(select.shape, BF16),
            pltpu.VMEM((2, panels, rows, HALF), F32),
            pltpu.VMEM((2, panels, rows, HALF), F32),
            pltpu.VMEM((2, 2, SIDE, HALF), F32),
            pltpu.VMEM((3, 2, 2, SIDE, HALF), F32),
            pltpu.VMEM((9, SIDE, SIDE), BF16),
            pltpu.VMEM((9, SIDE, SIDE), BF16),
            pltpu.VMEM((4, SIDE, SIDE), F32),
            pltpu.VMEM((5, SIDE, SIDE), F32),
            pltpu.SMEM((measured.shape[0],), jnp.int32),
            pltpu.SemaphoreType.DMA((32,)),
            pltpu.SemaphoreType.DMA((2, 2)),
        ],
        compiler_params=pltpu.CompilerParams(vmem_limit_bytes=56 * 1024 * 1024),
        cost_estimate=pl.CostEstimate(flops=2**20, bytes_accessed=2**20, transcendentals=0),
    )(live, offsets.T, probe, probe_grad, jnp.asarray(tables), jnp.asarray(select), measured, *blocks)


ROW_AXES = ("z", "y_lo", "core")
COL_AXES = ("x", "y_hi")
NEAR_AXES = ("z", "core", "x")
FAR_AXES = ("y_lo", "y_hi")


def passed_along(block, axes, distance):
    devices = range(lax.axis_size(axes))
    route = [(i - distance, i) for i in devices if i - distance in devices]
    return lax.ppermute(block, axes, route)


def passed_across(block, distance):
    rows, cols = lax.axis_size(ROW_AXES), lax.axis_size(COL_AXES)
    pairs = []
    for i in range(rows):
        for j in range(cols):
            if 0 <= i - distance < rows and 0 <= j - distance < cols:
                pairs.append(((i - distance) * cols + j - distance, i * cols + j))
    return lax.ppermute(block, ROW_AXES + COL_AXES, pairs)


def update_kernel(tile, own, from_left, above_left, above_right, across, out):
    top, low = pl.ds(0, SIDE), pl.ds(SIDE, TILE - SIDE)
    first, second = pl.ds(0, SIDE), pl.ds(SIDE, TILE - SIDE)
    for part in range(2):
        out[part, top, first] = tile[part, top, first] - 0.25 * (
            (own[part, top, first] + from_left[part, top, :]) + (above_left[part] + across[part])
        )
        out[part, low, first] = tile[part, low, first] - 0.25 * (own[part, low, first] + from_left[part, low, :])
        out[part, top, second] = tile[part, top, second] - 0.25 * (own[part, top, second] + above_right[part])
        out[part, low, second] = tile[part, low, second] - 0.25 * own[part, low, second]


def update(tile, *parts):
    return pl.pallas_call(
        update_kernel,
        out_shape=jax.ShapeDtypeStruct(tile.shape, F32),
        compiler_params=pltpu.CompilerParams(vmem_limit_bytes=32 * 1024 * 1024),
        cost_estimate=pl.CostEstimate(flops=2**20, bytes_accessed=2**20, transcendentals=0),
    )(tile, *parts)


def total_over_all(x):
    near = lax.axis_size(NEAR_AXES)
    blocks = x.reshape(-1, 8, HALF)
    shares = lax.all_to_all(blocks, NEAR_AXES, 0, 0, tiled=True)
    share = jnp.sum(shares.reshape(near, -1, 8, HALF), axis=0)
    far = lax.axis_size(FAR_AXES)
    others = [lax.ppermute(share, FAR_AXES, [(i, i ^ bits) for i in range(far)]) for bits in range(1, far)]
    share = (share + others[0]) + (others[1] + others[2])
    copies = jnp.broadcast_to(share[None], (near,) + share.shape).reshape(blocks.shape)
    return lax.all_to_all(copies, NEAR_AXES, 0, 0, tiled=True).reshape(x.shape)


def body(object_field, probe, measured, offsets, live):
    side = probe.shape[1]
    half = side // 2
    positions = measured.shape[0] * lax.axis_size(ROW_AXES) * lax.axis_size(COL_AXES)
    below = passed_along(object_field[:, :side, :], ROW_AXES, -1)
    right = passed_along(object_field[:, :, :side], COL_AXES, -1)
    corner = passed_across(object_field[:, :side, :side], -1)

    def call(plan, probe_grad, blocks):
        return slots_call(plan, live, offsets, probe, probe_grad, measured, blocks)

    grad_own, probe_grad = call(PLAN_OWN, jnp.zeros((2, 2, 8, half), F32), [object_field])
    below, right, corner, grad_own = lax.optimization_barrier((below, right, corner, grad_own))
    to_across, to_right, below_left, below_right, own_grad, probe_grad = call(
        PLAN_OUTER, probe_grad, [object_field, below, right, corner, grad_own]
    )
    from_left = passed_along(to_right, COL_AXES, 1)
    above_left = passed_along(below_left, ROW_AXES, 1)
    above_right = passed_along(below_right, ROW_AXES, 1)
    from_across = passed_across(to_across, 1)
    total_grad = total_over_all(probe_grad)
    object_next = update(object_field, own_grad, from_left, above_left, above_right, from_across)
    object_next, total_grad = lax.optimization_barrier((object_next, total_grad))
    total_grad = jnp.concatenate([total_grad[:, 0], total_grad[:, 1]], axis=2)
    probe_next = probe - (1.0 / math.sqrt(positions)) * total_grad
    return (object_next, probe_next)


def solution(mesh):
    whole = jax.sharding.Mesh(mesh.devices.reshape(4, 2, 2, 4, 2), ROW_AXES + COL_AXES)
    both = ROW_AXES + COL_AXES
    placed = (P(None, ROW_AXES, COL_AXES), P(), P(both, None), P(both), P(both))
    return jax.shard_map(
        body, mesh=whole, in_specs=placed, out_specs=(P(None, ROW_AXES, COL_AXES), P()), check_vma=False
    )
```

time: 169 us -> 151 us (0.89)
  blocking collectives: 38 us -> 0 us
  starting transfers between devices: 34.1 us -> 58.6 us
  waiting for transfers between devices: 33.1 us -> 47.3 us
  local copies, waits for them, and re-layouts: 16.8 us -> 8.12 us
  other arithmetic: 10.5 us -> 3.02 us
    all_to_all x1 -> x0, blocking collectives: 38 us -> none  [total_over_all(): return lax.all_to_all(copies, axes, 0, 0, tiled=True).reshape(x.shape)]
    ppermute x6 -> x10, starting transfers between devices: 18.7 us -> 35.2 us  [the longest x5 20.4 us: passed_along(): return lax.ppermute(block, axes, route)]
    all_to_all x1 -> x2, waiting for transfers between devices: 2.15 us -> 14.6 us  [the longest x1 7.56 us: total_over_all(): shares = lax.all_to_all(blocks, NEAR_AXES, 0, 0, tiled=True)]
    unnamed x31 -> x12, local copies, waits for them, and re-layouts: 11.4 us -> 3.14 us
    all_to_all x1 -> x2, starting transfers between devices: 15.4 us -> 23.4 us  [the longest x1 15.2 us: total_over_all(): shares = lax.all_to_all(blocks, NEAR_AXES, 0, 0, tiled=True)]
    scatter-add x3 -> x0, other arithmetic: 5.23 us -> none  [the longest x2 3.14 us: body(): own_grad.at[:, :side, :].add(from_above).at[:, :, :side].add(from_left)]
    mul x1 -> x0, other arithmetic: 2.29 us -> none  [body(): probe_next = probe - 1.0 / math.sqrt(positions) * total_grad]
    squeeze x0 -> x2, local copies, waits for them, and re-layouts: none -> 1.94 us  [body(): total_grad = jnp.concatenate([total_grad[:, 0], total_grad[:, 1]], axis=2)]
  transfers between devices with their start and end apart: 7 -> 12, of which waited for: 4 -> 5; matrix products, arithmetic and copies ran while one was open for 6% -> 2% of each run, Pallas kernels for 0% -> 10%
where the time goes in v2:
time: 151 us; the launch traced here: 150 us
  starting transfers between devices  58.6 us (39%)
  waiting for transfers between devices  47.3 us (31%)
  Pallas kernels  31.6 us (21%)
  local copies, waits for them, and re-layouts  8.12 us (5%)
  other arithmetic  3.02 us (2%)
    pallas_call x2, Pallas kernels, slots_call(): pl.pallas_call(functools.partial(slots_kernel, plan), out_shape=[jax.Shap...  28.6 us
    ppermute x2, waiting for transfers between devices, passed_across(): return lax.ppermute(block, ROW_AXES + COL_AXES, pairs)  26.6 us
    ppermute x5, starting transfers between devices, passed_along(): return lax.ppermute(block, axes, route)  20.4 us
    all_to_all x1, starting transfers between devices, total_over_all(): shares = lax.all_to_all(blocks, NEAR_AXES, 0, 0, tiled=True)  15.2 us
    all_to_all x1, starting transfers between devices, total_over_all(): return lax.all_to_all(copies, NEAR_AXES, 0, 0, tiled=True).reshape(x.shape)  8.18 us
    ppermute x2, starting transfers between devices, passed_across(): return lax.ppermute(block, ROW_AXES + COL_AXES, pairs)  7.96 us
    all_to_all x1, waiting for transfers between devices, total_over_all(): shares = lax.all_to_all(blocks, NEAR_AXES, 0, 0, tiled=True)  7.56 us
    all_to_all x1, waiting for transfers between devices, total_over_all(): return lax.all_to_all(copies, NEAR_AXES, 0, 0, tiled=True).reshape(x.shape)  7.06 us
  transfers between devices with their start and end apart: 12, of which 5 were waited for; matrix products, arithmetic and copies ran while one was open for 2% of the time, Pallas kernels for 10%

profile of v2, /device:TPU:25, one launch (start us, length us, event | category | flops | bytes accessed | tf_op | source)
XLA Modules:
  0.0 150.1 jit_solution(126758319915276660)
XLA Ops:
  0.6 0.0 copy-start
  0.6 1.4 slice.15
  2.1 2.6 %collective-permute-start = (f32[2,256,512]{2,1,0:T(8,128)S(1)}, f32[2,256,512]{2,1,0:T(8,128)S(1)}, u32[]{:S(2)}, u32[]{:S(2)}) collective-permute-start(f32[2,256,512]{2,1,0:T(8,128)S(1)} %slice.15), channel_id=1, source_target_pairs={{8,0},{16,8},{24,16},{32,24},{40,32},{48,40},{56,48},{64,56},{72,6... | collective-permute-start | bytes 3145736 | tf_op jit(solution)/shard_map/ppermute | solution.py:383
  4.7 0.0 copy-done
  4.7 0.1 slice.16
  4.8 2.9 %collective-permute-start.1 = (f32[2,512,256]{2,1,0:T(8,128)S(1)}, f32[2,512,256]{2,1,0:T(8,128)S(1)}, u32[]{:S(2)}, u32[]{:S(2)}) collective-permute-start(f32[2,512,256]{2,1,0:T(8,128)S(1)} %slice.16), channel_id=1, source_target_pairs={{1,0},{2,1},{3,2},{4,3},{5,4},{6,5},{7,6},{9,8},{10,9},{11,10},{12... | collective-permute-start | bytes 3145736 | tf_op jit(solution)/shard_map/ppermute | solution.py:383
  7.7 1.9 %collective-permute-start.2 = (f32[2,256,256]{2,1,0:T(8,128)S(1)}, f32[2,256,256]{2,1,0:T(8,128)S(1)}, u32[]{:S(2)}, u32[]{:S(2)}) collective-permute-start(f32[2,256,256]{2,1,0:T(8,128)S(1)} %slice.17), channel_id=1, source_target_pairs={{9,0},{10,1},{11,2},{12,3},{13,4},{14,5},{15,6},{17,8},{18,9},{19,... | collective-permute-start | bytes 1572872 | tf_op jit(solution)/shard_map/ppermute | solution.py:393
  10.3 0.6 broadcast_in_dim.4.refs_3_
  10.9 11.5 %shard_map.104 = (f32[2,4,512,128]{3,2,1,0:T(8,128)}, f32[2,2,256,128]{3,2,1,0:T(8,128)}) custom-call(s32[1]{0:T(128)S(6)} %copy.14.refs_0_, s32[2,16]{1,0:T(2,128)} %bitcast.11, f32[2,256,256]{2,1,0:T(8,128)} %refs_2_.3, f32[2,2,8,128]{3,2,1,0:T(8,128)} %broadcast_in_dim.4.refs_3_, bf16[2,2,2,256,256]{4,3,2,1,0:T(8,128)(2,1)} %constant.3.clone.refs_4_, ...), custom_call_target="tpu_custom_call" | custom-call | flops 1048576 | bytes 1048576 | tf_op jit(solution)/shard_map/pallas_call | solution.py:347
  22.4 24.3 %collective-permute-done.2.refs_10_ = f32[2,256,256]{2,1,0:T(8,128)S(1)} collective-permute-done((f32[2,256,256]{2,1,0:T(8,128)S(1)}, f32[2,256,256]{2,1,0:T(8,128)S(1)}, u32[]{:S(2)}, u32[]{:S(2)}) %collective-permute-start.2) | collective-permute-done | bytes 524320 | tf_op jit(solution)/shard_map/ppermute | solution.py:393
  46.7 0.0 copy-start.5
  46.7 0.0 collective-permute-done.refs_8_
  46.7 0.0 copy-start.3
  46.7 0.0 collective-permute-done.1.refs_9_
  46.7 0.0 copy-start.4
  46.7 0.8 copy-done.5
  47.5 0.4 copy-done.3
  47.9 0.4 copy-done.4
  48.2 17.1 %shard_map.105 = (f32[2,256,256]{2,1,0:T(8,128)}, f32[2,512,256]{2,1,0:T(8,128)}, f32[2,256,256]{2,1,0:T(8,128)}, f32[2,256,256]{2,1,0:T(8,128)}, f32[2,512,512]{2,1,0:T(8,128)}, /*index=5*/f32[2,2,256,128]{3,2,1,0:T(8,128)}) custom-call(s32[1]{0:T(128)S(6)} %copy.14.refs_0_, s32[2,16]{1,0:T(2,128)} %bitcast.12, f32[2,256,256]{2,1,0:T(8,128)} %refs_2_.3, ...), custom_call_target="tpu_custom_call" | custom-call | flops 1048576 | bytes 1048576 | tf_op jit(solution)/shard_map/pallas_call | solution.py:347
  65.3 0.0 copy-start.1
  65.4 15.2 %all-to-all-start = ((f32[128,8,128]{2,1,0:T(8,128)}), f32[128,8,128]{2,1,0:T(8,128)}, u32[]{:S(2)}, u32[]{:S(2)}) async-start(f32[128,8,128]{2,1,0:T(8,128)} %bitcast.10), calls=%async_computation | async-start | bytes 1048576 | tf_op jit(solution)/shard_map/all_to_all | solution.py:420
  80.6 3.9 %collective-permute-start.3 = (f32[2,512,256]{2,1,0:T(8,128)}, f32[2,512,256]{2,1,0:T(8,128)S(1)}, u32[]{:S(2)}, u32[]{:S(2)}) collective-permute-start(f32[2,512,256]{2,1,0:T(8,128)} %get-tuple-element.23), channel_id=1, source_target_pairs={{0,1},{1,2},{2,3},{3,4},{4,5},{5,6},{6,7},{8,9},{9,10},{10,11},{11... | collective-permute-start | bytes 3145736 | tf_op jit(solution)/shard_map/ppermute | solution.py:383
  84.5 7.6 %all-to-all-done = f32[128,8,128]{2,1,0:T(8,128)} async-done(((f32[128,8,128]{2,1,0:T(8,128)}), f32[128,8,128]{2,1,0:T(8,128)}, u32[]{:S(2)}, u32[]{:S(2)}) %all-to-all-start) | async-done | bytes 524320 | tf_op jit(solution)/shard_map/all_to_all | solution.py:420
  92.0 1.1 reduce_sum.9
  93.1 5.5 %collective-permute-start.9 = (f32[4,8,128]{2,1,0:T(8,128)S(1)}, f32[4,8,128]{2,1,0:T(8,128)S(1)}, u32[]{:S(2)}, u32[]{:S(2)}) collective-permute-start(f32[4,8,128]{2,1,0:T(8,128)S(1)} %reduce_sum.9), channel_id=1, source_target_pairs={{0,17},{1,16},{16,1},{17,0},{2,19},{3,18},{18,3},{19,2},{4,21},{5,... | collective-permute-start | bytes 49160 | tf_op jit(solution)/shard_map/ppermute | solution.py:423
  98.6 0.0 collective-permute-start.8
  98.6 1.3 collective-permute-start.7
  99.9 3.5 %collective-permute-start.4 = (f32[2,256,256]{2,1,0:T(8,128)}, f32[2,256,256]{2,1,0:T(8,128)}, u32[]{:S(2)}, u32[]{:S(2)}) collective-permute-start(f32[2,256,256]{2,1,0:T(8,128)} %get-tuple-element.24), channel_id=1, source_target_pairs={{0,8},{8,16},{16,24},{24,32},{32,40},{40,48},{48,56},{56,64},{64,7... | collective-permute-start | bytes 1572872 | tf_op jit(solution)/shard_map/ppermute | solution.py:383
  103.4 6.1 %collective-permute-done.9 = f32[4,8,128]{2,1,0:T(8,128)S(1)} collective-permute-done((f32[4,8,128]{2,1,0:T(8,128)S(1)}, f32[4,8,128]{2,1,0:T(8,128)S(1)}, u32[]{:S(2)}, u32[]{:S(2)}) %collective-permute-start.9) | collective-permute-done | bytes 16416 | tf_op jit(solution)/shard_map/ppermute | solution.py:423
  109.5 7.6 %collective-permute-start.5 = (f32[2,256,256]{2,1,0:T(8,128)}, f32[2,256,256]{2,1,0:T(8,128)}, u32[]{:S(2)}, u32[]{:S(2)}) collective-permute-start(f32[2,256,256]{2,1,0:T(8,128)} %get-tuple-element.25), channel_id=1, source_target_pairs={{0,8},{8,16},{16,24},{24,32},{32,40},{40,48},{48,56},{56,64},{64,7... | collective-permute-start | bytes 1572872 | tf_op jit(solution)/shard_map/ppermute | solution.py:383
  117.1 0.0 collective-permute-done.8
  117.2 6.0 %collective-permute-start.6 = (f32[2,256,256]{2,1,0:T(8,128)}, f32[2,256,256]{2,1,0:T(8,128)}, u32[]{:S(2)}, u32[]{:S(2)}) collective-permute-start(f32[2,256,256]{2,1,0:T(8,128)} %get-tuple-element.26), channel_id=1, source_target_pairs={{0,9},{1,10},{2,11},{3,12},{4,13},{5,14},{6,15},{8,17},{9,18},{10,... | collective-permute-start | bytes 1572872 | tf_op jit(solution)/shard_map/ppermute | solution.py:393
  123.2 0.0 collective-permute-done.7
  123.2 0.9 broadcast_in_dim.10
  124.1 8.2 %all-to-all-start.1 = ((f32[128,8,128]{2,1,0:T(8,128)}), f32[128,8,128]{2,1,0:T(8,128)}, u32[]{:S(2)}, u32[]{:S(2)}) async-start(f32[128,8,128]{2,1,0:T(8,128)} %bitcast.9), calls=%async_computation.1 | async-start | bytes 1048576 | tf_op jit(solution)/shard_map/all_to_all | solution.py:426
  132.3 0.0 collective-permute-done.4.above_left
  132.3 0.0 collective-permute-done.5.above_right
  132.3 2.3 %collective-permute-done.6.across = f32[2,256,256]{2,1,0:T(8,128)} collective-permute-done((f32[2,256,256]{2,1,0:T(8,128)}, f32[2,256,256]{2,1,0:T(8,128)}, u32[]{:S(2)}, u32[]{:S(2)}) %collective-permute-start.6) | collective-permute-done | bytes 524320 | tf_op jit(solution)/shard_map/ppermute | solution.py:393
  134.5 0.0 collective-permute-done.3.from_left
  134.5 0.0 copy-done.1
  134.5 0.0 copy-start.2
  134.5 1.6 %copy-done.2 = f32[2,512,512]{2,1,0:T(8,128)S(1)} copy-done((f32[2,512,512]{2,1,0:T(8,128)S(1)}, f32[2,512,512]{2,1,0:T(8,128)}, u32[]{:S(2)}) %copy-start.2) | copy-done | bytes 2097176
  136.1 3.0 %shard_map.106 = f32[2,512,512]{2,1,0:T(8,128)} custom-call(f32[2,512,512]{2,1,0:T(8,128)S(1)} %copy-done.1, f32[2,512,512]{2,1,0:T(8,128)S(1)} %copy-done.2, f32[2,512,256]{2,1,0:T(8,128)S(1)} %collective-permute-done.3.from_left, f32[2,256,256]{2,1,0:T(8,128)} %collective-permute-done.4.above_left, f32[2,256,256]{2,1,0:T(8,128)} %collective-permute-done.5.above_right, ...), custom_call_target="tpu_custom_call" | custom-call | flops 1048576 | bytes 1048576 | tf_op jit(solution)/shard_map/pallas_call | solution.py:409
  139.2 7.1 %all-to-all-done.1 = f32[128,8,128]{2,1,0:T(8,128)} async-done(((f32[128,8,128]{2,1,0:T(8,128)}), f32[128,8,128]{2,1,0:T(8,128)}, u32[]{:S(2)}, u32[]{:S(2)}) %all-to-all-start.1) | async-done | bytes 524320 | tf_op jit(solution)/shard_map/all_to_all | solution.py:426
  146.2 1.0 slice_bitcast_fusion.1
  147.2 1.0 slice_bitcast_fusion
  148.2 1.9 %fusion = f32[2,256,256]{2,1,0:T(8,128)} fusion(f32[2,256,256]{2,1,0:T(8,128)} %refs_2_.3, f32[2,256,128]{2,1,0:T(8,128)S(1)} %slice_bitcast_fusion.1, f32[2,256,128]{2,1,0:T(8,128)S(1)} %slice_bitcast_fusion), kind=kLoop, calls=%fused_computation.1 | loop fusion | flops 393216 | bytes 1572864 | tf_op jit(solution)/shard_map/sub | solution.py:453
  (2 shorter events, 0.0 us)
Async XLA Ops:
  0.6 4.1 %copy-start = (f32[2,512,512]{2,1,0:T(8,128)S(1)}, f32[2,512,512]{2,1,0:T(8,128)}, u32[]{:S(2)}) copy-start(f32[2,512,512]{2,1,0:T(8,128)} %tile.1) | copy-start | bytes 6291460
  2.1 44.6 %collective-permute-start = (f32[2,256,512]{2,1,0:T(8,128)S(1)}, f32[2,256,512]{2,1,0:T(8,128)S(1)}, u32[]{:S(2)}, u32[]{:S(2)}) collective-permute-start(f32[2,256,512]{2,1,0:T(8,128)S(1)} %slice.15), channel_id=1, source_target_pairs={{8,0},{16,8},{24,16},{32,24},{40,32},{48,40},{56,48},{64,56},{72,6... | collective-permute-start | bytes 3145736 | tf_op jit(solution)/shard_map/ppermute | solution.py:383
  4.8 41.9 %collective-permute-start.1 = (f32[2,512,256]{2,1,0:T(8,128)S(1)}, f32[2,512,256]{2,1,0:T(8,128)S(1)}, u32[]{:S(2)}, u32[]{:S(2)}) collective-permute-start(f32[2,512,256]{2,1,0:T(8,128)S(1)} %slice.16), channel_id=1, source_target_pairs={{1,0},{2,1},{3,2},{4,3},{5,4},{6,5},{7,6},{9,8},{10,9},{11,10},{12... | collective-permute-start | bytes 3145736 | tf_op jit(solution)/shard_map/ppermute | solution.py:383
  7.7 39.0 %collective-permute-start.2 = (f32[2,256,256]{2,1,0:T(8,128)S(1)}, f32[2,256,256]{2,1,0:T(8,128)S(1)}, u32[]{:S(2)}, u32[]{:S(2)}) collective-permute-start(f32[2,256,256]{2,1,0:T(8,128)S(1)} %slice.17), channel_id=1, source_target_pairs={{9,0},{10,1},{11,2},{12,3},{13,4},{14,5},{15,6},{17,8},{18,9},{19,... | collective-permute-start | bytes 1572872 | tf_op jit(solution)/shard_map/ppermute | solution.py:393
  46.7 0.8 copy-start.5
  46.7 1.2 copy-start.3
  46.7 1.5 %copy-start.4 = (f32[2,512,256]{2,1,0:T(8,128)}, f32[2,512,256]{2,1,0:T(8,128)S(1)}, u32[]{:S(2)}) copy-start(f32[2,512,256]{2,1,0:T(8,128)S(1)} %collective-permute-done.1.refs_9_) | copy-start | bytes 3145732
  65.3 69.2 %copy-start.1 = (f32[2,512,512]{2,1,0:T(8,128)S(1)}, f32[2,512,512]{2,1,0:T(8,128)}, u32[]{:S(2)}) copy-start(f32[2,512,512]{2,1,0:T(8,128)} %tile.1) | copy-start | bytes 6291460
  65.4 26.7 %all-to-all-start = ((f32[128,8,128]{2,1,0:T(8,128)}), f32[128,8,128]{2,1,0:T(8,128)}, u32[]{:S(2)}, u32[]{:S(2)}) async-start(f32[128,8,128]{2,1,0:T(8,128)} %bitcast.10), calls=%async_computation | async-start | bytes 1048576 | tf_op jit(solution)/shard_map/all_to_all | solution.py:420
  80.6 54.0 %collective-permute-start.3 = (f32[2,512,256]{2,1,0:T(8,128)}, f32[2,512,256]{2,1,0:T(8,128)S(1)}, u32[]{:S(2)}, u32[]{:S(2)}) collective-permute-start(f32[2,512,256]{2,1,0:T(8,128)} %get-tuple-element.23), channel_id=1, source_target_pairs={{0,1},{1,2},{2,3},{3,4},{4,5},{5,6},{6,7},{8,9},{9,10},{10,11},{11... | collective-permute-start | bytes 3145736 | tf_op jit(solution)/shard_map/ppermute | solution.py:383
  93.1 16.4 %collective-permute-start.9 = (f32[4,8,128]{2,1,0:T(8,128)S(1)}, f32[4,8,128]{2,1,0:T(8,128)S(1)}, u32[]{:S(2)}, u32[]{:S(2)}) collective-permute-start(f32[4,8,128]{2,1,0:T(8,128)S(1)} %reduce_sum.9), channel_id=1, source_target_pairs={{0,17},{1,16},{16,1},{17,0},{2,19},{3,18},{18,3},{19,2},{4,21},{5,... | collective-permute-start | bytes 49160 | tf_op jit(solution)/shard_map/ppermute | solution.py:423
  98.6 18.5 %collective-permute-start.8 = (f32[4,8,128]{2,1,0:T(8,128)S(1)}, f32[4,8,128]{2,1,0:T(8,128)S(1)}, u32[]{:S(2)}, u32[]{:S(2)}) collective-permute-start(f32[4,8,128]{2,1,0:T(8,128)S(1)} %reduce_sum.9), channel_id=1, source_target_pairs={{0,16},{1,17},{16,0},{17,1},{2,18},{3,19},{18,2},{19,3},{4,20},{5,... | collective-permute-start | bytes 49160 | tf_op jit(solution)/shard_map/ppermute | solution.py:423
  98.6 24.6 %collective-permute-start.7 = (f32[4,8,128]{2,1,0:T(8,128)S(1)}, f32[4,8,128]{2,1,0:T(8,128)S(1)}, u32[]{:S(2)}, u32[]{:S(2)}) collective-permute-start(f32[4,8,128]{2,1,0:T(8,128)S(1)} %reduce_sum.9), channel_id=1, source_target_pairs={{0,1},{1,0},{16,17},{17,16},{2,3},{3,2},{18,19},{19,18},{4,5},{5,4... | collective-permute-start | bytes 49160 | tf_op jit(solution)/shard_map/ppermute | solution.py:423
  99.9 32.4 %collective-permute-start.4 = (f32[2,256,256]{2,1,0:T(8,128)}, f32[2,256,256]{2,1,0:T(8,128)}, u32[]{:S(2)}, u32[]{:S(2)}) collective-permute-start(f32[2,256,256]{2,1,0:T(8,128)} %get-tuple-element.24), channel_id=1, source_target_pairs={{0,8},{8,16},{16,24},{24,32},{32,40},{40,48},{48,56},{56,64},{64,7... | collective-permute-start | bytes 1572872 | tf_op jit(solution)/shard_map/ppermute | solution.py:383
  109.5 22.8 %collective-permute-start.5 = (f32[2,256,256]{2,1,0:T(8,128)}, f32[2,256,256]{2,1,0:T(8,128)}, u32[]{:S(2)}, u32[]{:S(2)}) collective-permute-start(f32[2,256,256]{2,1,0:T(8,128)} %get-tuple-element.25), channel_id=1, source_target_pairs={{0,8},{8,16},{16,24},{24,32},{32,40},{40,48},{48,56},{56,64},{64,7... | collective-permute-start | bytes 1572872 | tf_op jit(solution)/shard_map/ppermute | solution.py:383
  117.2 17.4 %collective-permute-start.6 = (f32[2,256,256]{2,1,0:T(8,128)}, f32[2,256,256]{2,1,0:T(8,128)}, u32[]{:S(2)}, u32[]{:S(2)}) collective-permute-start(f32[2,256,256]{2,1,0:T(8,128)} %get-tuple-element.26), channel_id=1, source_target_pairs={{0,9},{1,10},{2,11},{3,12},{4,13},{5,14},{6,15},{8,17},{9,18},{10,... | collective-permute-start | bytes 1572872 | tf_op jit(solution)/shard_map/ppermute | solution.py:393
  124.1 22.1 %all-to-all-start.1 = ((f32[128,8,128]{2,1,0:T(8,128)}), f32[128,8,128]{2,1,0:T(8,128)}, u32[]{:S(2)}, u32[]{:S(2)}) async-start(f32[128,8,128]{2,1,0:T(8,128)} %bitcast.9), calls=%async_computation.1 | async-start | bytes 1048576 | tf_op jit(solution)/shard_map/all_to_all | solution.py:426
  134.5 1.6 %copy-start.2 = (f32[2,512,512]{2,1,0:T(8,128)S(1)}, f32[2,512,512]{2,1,0:T(8,128)}, u32[]{:S(2)}) copy-start(f32[2,512,512]{2,1,0:T(8,128)} %get-tuple-element.22.own) | copy-start | bytes 6291460

commit v3 on v2

--- a/solution.py
+++ b/solution.py
@@ -62,8 +62,8 @@
     return mm(x_high, high) + (mm(x_low, high) + mm(x_high, low))
 
 
-def cut_steps(r, c, ext, probe, patch, xh, xl):
-    j = c // HALF
+def cut_steps(r, c, base, ext, probe, patch, xh, xl):
+    j = c // HALF - base
     back_shift = lax.rem(HALF - c % HALF, HALF)
     lane = lax.broadcasted_iota(jnp.int32, (ROWS, HALF), 1)
     take_first = lane < HALF - c % HALF
@@ -160,8 +160,8 @@
     return first, middle
 
 
-def grad_steps(r, c, grad, probe, pgrad, patch, fb):
-    j = c // HALF
+def grad_steps(r, c, base, grad, probe, pgrad, patch, fb):
+    j = c // HALF - base
     s = c % HALF
     lane = lax.broadcasted_iota(jnp.int32, (ROWS, HALF), 1)
     below_shift = lane < s
@@ -214,11 +214,11 @@
     slots = measured.shape[0]
 
     early, late = [(probe_in, probe)], [(tab_in, tab), (sel_in, sel)]
-    if plan["keep"]:
+    if plan["first"]:
         pgrad[...] = jnp.zeros_like(pgrad)
     else:
         late.append((pgrad_in, pgrad))
-    for (kind, panel, row, panels), block in zip(plan["in"], blocks):
+    for (kind, panel, row, panels, source, rows), block in zip(plan["in"], blocks):
         if kind == "grad":
             late.append((block, grad.at[:, pl.ds(panel, panels), pl.ds(row, block.shape[2]), :]))
             continue
@@ -226,8 +226,8 @@
             first = block.shape[2] // HALF - panels
             for h in range(panels):
                 early.append((
-                    block.at[part, :, pl.ds((first + h) * HALF, HALF)],
-                    ext.at[part, panel + h, pl.ds(row, block.shape[1]), :],
+                    block.at[part, pl.ds(source, rows), pl.ds((first + h) * HALF, HALF)],
+                    ext.at[part, panel + h, pl.ds(row, rows), :],
                 ))
     loads = [pltpu.make_async_copy(*pair, sems.at[i]) for i, pair in enumerate(early + late)]
     for load in loads:
@@ -238,8 +238,8 @@
     def collect(g, n):
         order[n] = g
         r, c = offsets[0, g], offsets[1, g]
-        inside = (r <= TILE - SIDE) & (c <= TILE - SIDE)
-        used = (g < live[0]) & (inside if plan["keep"] else ~inside)
+        low_r, high_r, low_c, high_c = plan["keep"]
+        used = (g < live[0]) & (r >= low_r) & (r <= high_r) & (c >= low_c) & (c <= high_c)
         return n + used.astype(jnp.int32)
 
     total = lax.fori_loop(0, slots, collect, jnp.int32(0))
@@ -268,7 +268,7 @@
         fb[pl.ds(3, 2)] = jnp.zeros((2, SIDE, SIDE), F32)
         patch[2] = jnp.zeros((2, 2, SIDE, HALF), F32)
         r, c = place(0)
-        for run in cut_steps(r, c, ext, probe, patch.at[0], xh, xl):
+        for run in cut_steps(r, c, plan["base"], ext, probe, patch.at[0], xh, xl):
             run()
         for load in loads[len(early):]:
             load.wait()
@@ -284,15 +284,15 @@
             first, middle = transform_steps(meas.at[lax.rem(n, 2)], tab, sel, xh, xl, fa, fb)
             r, c = place(jnp.maximum(n - 1, 0))
             interleaved(
-                first, grad_steps(r, c, grad, probe, pgrad, patch.at[lax.rem(n + 2, 3)], fb)
+                first, grad_steps(r, c, plan["base"], grad, probe, pgrad, patch.at[lax.rem(n + 2, 3)], fb)
             )
             r, c = place(jnp.minimum(n + 1, total - 1))
-            interleaved(middle, cut_steps(r, c, ext, probe, patch.at[lax.rem(n + 1, 3)], xh, xl))
+            interleaved(middle, cut_steps(r, c, plan["base"], ext, probe, patch.at[lax.rem(n + 1, 3)], xh, xl))
             return carry
 
         lax.fori_loop(0, total, step, 0)
         r, c = place(total - 1)
-        for run in grad_steps(r, c, grad, probe, pgrad, patch.at[lax.rem(total + 2, 3)], fb):
+        for run in grad_steps(r, c, plan["base"], grad, probe, pgrad, patch.at[lax.rem(total + 2, 3)], fb):
             run()
 
     @pl.when(total == 0)
@@ -322,19 +322,30 @@
 
 
 PLAN_OWN = {
-    "panels": 5, "keep": True,
-    "in": [("ext", 0, 0, 4)],
+    "base": 0, "panels": 5, "keep": (0, SIDE, 0, SIDE), "first": True,
+    "in": [("ext", 0, 0, 4, 0, TILE)],
     "zero": [(0, 4, 0, TILE)],
-    "out": [("grad", 0, 0, 4)], "shapes": [(2, 4, TILE, HALF)],
+    "out": [("array", 0, 0, 2), ("grad", 0, SIDE, 2), ("grad", 2, 0, 2)],
+    "shapes": [(2, SIDE, SIDE), (2, 2, SIDE, HALF), (2, 2, TILE, HALF)],
 }
-PLAN_OUTER = {
-    "panels": 6, "keep": False,
-    "in": [("ext", 0, 0, 4), ("ext", 0, TILE, 4), ("ext", 4, 0, 2), ("ext", 4, TILE, 2), ("grad", 0, 0, 4)],
-    "zero": [(0, 4, TILE, SIDE), (4, 2, 0, WIDE)],
+PLAN_RIGHT = {
+    "base": 2, "panels": 4, "keep": (0, SIDE, SIDE + 1, TILE), "first": False,
+    "in": [("ext", 0, 0, 2, 0, TILE), ("ext", 2, 0, 2, 0, TILE), ("grad", 0, 0, 2, 0, TILE)],
+    "zero": [(2, 2, 0, TILE)],
+    "out": [("array", 0, 0, 2), ("array", 2, 0, 2), ("grad", 0, SIDE, 4)],
+    "shapes": [(2, SIDE, SIDE), (2, SIDE, SIDE), (2, 4, SIDE, HALF)],
+}
+PLAN_LOWER = {
+    "base": 0, "panels": 6, "keep": (SIDE + 1, TILE, 0, TILE), "first": False,
+    "in": [
+        ("ext", 0, SIDE, 4, SIDE, SIDE), ("ext", 0, TILE, 4, 0, SIDE), ("ext", 4, SIDE, 2, SIDE, SIDE),
+        ("ext", 4, TILE, 2, 0, SIDE), ("grad", 0, SIDE, 2, 0, SIDE), ("grad", 2, SIDE, 4, 0, SIDE),
+    ],
+    "zero": [(0, 6, TILE, SIDE)],
     "out": [
-        ("array", 4, TILE, 2), ("array", 4, 0, 2), ("array", 0, TILE, 2), ("array", 2, TILE, 2), ("array", 0, 0, 4),
+        ("array", 4, TILE, 2), ("array", 4, SIDE, 2), ("array", 0, TILE, 2), ("array", 2, TILE, 2), ("array", 0, SIDE, 4),
     ],
-    "shapes": [(2, SIDE, SIDE), (2, TILE, SIDE), (2, SIDE, SIDE), (2, SIDE, SIDE), (2, TILE, TILE)],
+    "shapes": [(2, SIDE, SIDE), (2, SIDE, SIDE), (2, SIDE, SIDE), (2, SIDE, SIDE), (2, SIDE, TILE)],
 }
 
 
@@ -393,16 +404,16 @@
     return lax.ppermute(block, ROW_AXES + COL_AXES, pairs)
 
 
-def update_kernel(tile, own, from_left, above_left, above_right, across, out):
+def update_kernel(tile, top_left, top_right, lower, left_top, left_low, above_left, above_right, across, out):
     top, low = pl.ds(0, SIDE), pl.ds(SIDE, TILE - SIDE)
     first, second = pl.ds(0, SIDE), pl.ds(SIDE, TILE - SIDE)
     for part in range(2):
         out[part, top, first] = tile[part, top, first] - 0.25 * (
-            (own[part, top, first] + from_left[part, top, :]) + (above_left[part] + across[part])
+            (top_left[part] + left_top[part]) + (above_left[part] + across[part])
         )
-        out[part, low, first] = tile[part, low, first] - 0.25 * (own[part, low, first] + from_left[part, low, :])
-        out[part, top, second] = tile[part, top, second] - 0.25 * (own[part, top, second] + above_right[part])
-        out[part, low, second] = tile[part, low, second] - 0.25 * own[part, low, second]
+        out[part, top, second] = tile[part, top, second] - 0.25 * (top_right[part] + above_right[part])
+        out[part, low, first] = tile[part, low, first] - 0.25 * (lower[part, :, first] + left_low[part])
+        out[part, low, second] = tile[part, low, second] - 0.25 * lower[part, :, second]
 
 
 def update(tile, *parts):
@@ -414,43 +425,67 @@
     )(tile, *parts)
 
 
-def total_over_all(x):
+def probe_kernel(scale, probe, total, out):
+    for part in range(2):
+        for h in range(2):
+            cols = pl.ds(h * HALF, HALF)
+            out[part, :, cols] = probe[part, :, cols] - scale * total[part, h]
+
+
+def probe_update(scale, probe, total):
+    return pl.pallas_call(
+        functools.partial(probe_kernel, scale),
+        out_shape=jax.ShapeDtypeStruct(probe.shape, F32),
+        cost_estimate=pl.CostEstimate(flops=2**20, bytes_accessed=2**20, transcendentals=0),
+    )(probe, total)
+
+
+def total_over_all(x, before):
     near = lax.axis_size(NEAR_AXES)
     blocks = x.reshape(-1, 8, HALF)
     shares = lax.all_to_all(blocks, NEAR_AXES, 0, 0, tiled=True)
     share = jnp.sum(shares.reshape(near, -1, 8, HALF), axis=0)
     far = lax.axis_size(FAR_AXES)
-    others = [lax.ppermute(share, FAR_AXES, [(i, i ^ bits) for i in range(far)]) for bits in range(1, far)]
-    share = (share + others[0]) + (others[1] + others[2])
+    copies = jnp.broadcast_to(share[None], (far,) + share.shape).reshape((-1,) + share.shape[1:])
+    share = lax.all_to_all(copies, FAR_AXES, 0, 0, tiled=True)
+    share = jnp.sum(share.reshape((far, -1) + share.shape[1:]), axis=0)
+    share, before = lax.optimization_barrier((share, before))
     copies = jnp.broadcast_to(share[None], (near,) + share.shape).reshape(blocks.shape)
-    return lax.all_to_all(copies, NEAR_AXES, 0, 0, tiled=True).reshape(x.shape)
+    return lax.all_to_all(copies, NEAR_AXES, 0, 0, tiled=True).reshape(x.shape), before
 
 
 def body(object_field, probe, measured, offsets, live):
     side = probe.shape[1]
     half = side // 2
     positions = measured.shape[0] * lax.axis_size(ROW_AXES) * lax.axis_size(COL_AXES)
-    below = passed_along(object_field[:, :side, :], ROW_AXES, -1)
     right = passed_along(object_field[:, :, :side], COL_AXES, -1)
-    corner = passed_across(object_field[:, :side, :side], -1)
 
     def call(plan, probe_grad, blocks):
         return slots_call(plan, live, offsets, probe, probe_grad, measured, blocks)
 
-    grad_own, probe_grad = call(PLAN_OWN, jnp.zeros((2, 2, 8, half), F32), [object_field])
-    below, right, corner, grad_own = lax.optimization_barrier((below, right, corner, grad_own))
-    to_across, to_right, below_left, below_right, own_grad, probe_grad = call(
-        PLAN_OUTER, probe_grad, [object_field, below, right, corner, grad_own]
+    top_left, grad_left, grad_right, probe_grad = call(PLAN_OWN, jnp.zeros((2, 2, 8, half), F32), [object_field])
+    below_source, corner_source, grad_right = lax.optimization_barrier(
+        (object_field[:, :side, :], object_field[:, :side, :side], grad_right)
     )
-    from_left = passed_along(to_right, COL_AXES, 1)
+    below = passed_along(below_source, ROW_AXES, -1)
+    corner = passed_across(corner_source, -1)
+    top_right, right_top, grad_low, probe_grad = call(PLAN_RIGHT, probe_grad, [object_field, right, grad_right])
+    below, corner, grad_low, right_top = lax.optimization_barrier((below, corner, grad_low, right_top))
+    left_top = passed_along(right_top, COL_AXES, 1)
+    to_across, right_low, below_left, below_right, lower, probe_grad = call(
+        PLAN_LOWER, probe_grad, [object_field, below, right, corner, grad_left, grad_low]
+    )
+    from_across = passed_across(to_across, 1)
     above_left = passed_along(below_left, ROW_AXES, 1)
     above_right = passed_along(below_right, ROW_AXES, 1)
-    from_across = passed_across(to_across, 1)
-    total_grad = total_over_all(probe_grad)
-    object_next = update(object_field, own_grad, from_left, above_left, above_right, from_across)
+    left_top, probe_grad = lax.optimization_barrier((left_top, probe_grad))
+    total_grad, (from_across, right_low) = total_over_all(probe_grad, (from_across, right_low))
+    left_low = passed_along(right_low, COL_AXES, 1)
+    object_next = update(
+        object_field, top_left, top_right, lower, left_top, left_low, above_left, above_right, from_across
+    )
     object_next, total_grad = lax.optimization_barrier((object_next, total_grad))
-    total_grad = jnp.concatenate([total_grad[:, 0], total_grad[:, 1]], axis=2)
-    probe_next = probe - (1.0 / math.sqrt(positions)) * total_grad
+    probe_next = probe_update(1.0 / math.sqrt(positions), probe, total_grad)
     return (object_next, probe_next)
 
 

time: 151 us -> 139 us (0.921)
  Pallas kernels: 31.6 us -> 24.7 us
  waiting for transfers between devices: 47.3 us -> 41.5 us
  starting transfers between devices: 58.6 us -> 61.8 us
  other arithmetic: 3.02 us -> 1.1 us
    ppermute x5 -> x6, waiting for transfers between devices: 0.01 us -> 30.6 us  [passed_along(): return lax.ppermute(block, axes, route)]
    ppermute x2, waiting for transfers between devices: 26.6 us -> 6.95 us  [passed_across(): return lax.ppermute(block, ROW_AXES + COL_AXES, pairs)]
    all_to_all x1 -> x2, starting transfers between devices: 8.18 us -> 18 us  [the longest x1 11 us: total_over_all(): share = lax.all_to_all(copies, FAR_AXES, 0, 0, tiled=True)]
    pallas_call x2 -> x3, Pallas kernels: 28.6 us -> 19.5 us  [slots_call(): pl.pallas_call(functools.partial(slots_kernel, plan), out_shape=[jax.Shap...]
    all_to_all x1 -> x2, waiting for transfers between devices: 7.06 us -> 0.01 us  [the longest x1 0.01 us: total_over_all(): share = lax.all_to_all(copies, FAR_AXES, 0, 0, tiled=True)]
    ppermute x3 -> x0, starting transfers between devices: 6.8 us -> none  [total_over_all(): lax.ppermute(share, FAR_AXES, [(i, i ^ bits) for i in range(far)])]
    ppermute x3 -> x0, waiting for transfers between devices: 6.09 us -> none  [total_over_all(): lax.ppermute(share, FAR_AXES, [(i, i ^ bits) for i in range(far)])]
    all_to_all x1, waiting for transfers between devices: 7.56 us -> 3.89 us  [total_over_all(): shares = lax.all_to_all(blocks, NEAR_AXES, 0, 0, tiled=True)]
  transfers between devices with their start and end apart: 12 -> 11, of which waited for: 5 -> 7; matrix products, arithmetic and copies ran while one was open for 2% -> 2% of each run, Pallas kernels for 10% -> 16%
where the time goes in v3:
time: 139 us
  starting transfers between devices  61.8 us (44%)
  waiting for transfers between devices  41.5 us (30%)
  Pallas kernels  24.7 us (18%)
  local copies, waits for them, and re-layouts  8.41 us (6%)
  between operations  1.48 us (1%)
    ppermute x6, waiting for transfers between devices, passed_along(): return lax.ppermute(block, axes, route)  30.6 us
    ppermute x6, starting transfers between devices, passed_along(): return lax.ppermute(block, axes, route)  19.6 us
    pallas_call x3, Pallas kernels, slots_call(): pl.pallas_call(functools.partial(slots_kernel, plan), out_shape=[jax.Shap...  19.5 us
    all_to_all x1, starting transfers between devices, total_over_all(): shares = lax.all_to_all(blocks, NEAR_AXES, 0, 0, tiled=True)  14.1 us
    all_to_all x1, starting transfers between devices, total_over_all(): share = lax.all_to_all(copies, FAR_AXES, 0, 0, tiled=True)  11 us
    ppermute x2, starting transfers between devices, passed_across(): return lax.ppermute(block, ROW_AXES + COL_AXES, pairs)  10.1 us
    all_to_all x1, starting transfers between devices, total_over_all(): lax.all_to_all(copies, NEAR_AXES, 0, 0, tiled=True).reshape(x.shape)  6.96 us
    ppermute x2, waiting for transfers between devices, passed_across(): return lax.ppermute(block, ROW_AXES + COL_AXES, pairs)  6.95 us
  transfers between devices with their start and end apart: 11, of which 7 were waited for; matrix products, arithmetic and copies ran while one was open for 2% of the time, Pallas kernels for 16%

profile of v3, /device:TPU:25, one launch (start us, length us, event | category | flops | bytes accessed | tf_op | source)
XLA Modules:
  0.0 139.0 jit_solution(4418560070678277164)
XLA Ops:
  0.6 1.3 slice.9
  1.9 2.9 %collective-permute-start = (f32[2,512,256]{2,1,0:T(8,128)S(1)}, f32[2,512,256]{2,1,0:T(8,128)S(1)}, u32[]{:S(2)}, u32[]{:S(2)}) collective-permute-start(f32[2,512,256]{2,1,0:T(8,128)S(1)} %slice.9), channel_id=1, source_target_pairs={{1,0},{2,1},{3,2},{4,3},{5,4},{6,5},{7,6},{9,8},{10,9},{11,10},{12... | collective-permute-start | bytes 3145736 | tf_op jit(solution)/shard_map/ppermute | solution.py:394
  5.4 0.6 broadcast_in_dim.6.refs_3_
  6.0 0.0 copy-start
  6.1 4.7 %shard_map.122 = (f32[2,256,256]{2,1,0:T(8,128)}, f32[2,2,256,128]{3,2,1,0:T(8,128)}, f32[2,2,512,128]{3,2,1,0:T(8,128)}, f32[2,2,256,128]{3,2,1,0:T(8,128)}) custom-call(s32[1]{0:T(128)S(6)} %copy.13.refs_0_, s32[2,16]{1,0:T(2,128)} %bitcast.10, f32[2,256,256]{2,1,0:T(8,128)} %probe.1, f32[2,2,8,128]{3,2,1,0:T(8,128)} %broadcast_in_dim.6.refs_3_, ...), custom_call_target="tpu_custom_call" | custom-call | flops 1048576 | bytes 1048576 | tf_op jit(solution)/shard_map/pallas_call | solution.py:358
  10.7 0.0 copy-done
  10.8 0.1 slice.10
  10.9 4.9 %collective-permute-start.1 = (f32[2,256,512]{2,1,0:T(8,128)S(1)}, f32[2,256,512]{2,1,0:T(8,128)S(1)}, u32[]{:S(2)}, u32[]{:S(2)}) collective-permute-start(f32[2,256,512]{2,1,0:T(8,128)S(1)} %slice.10), channel_id=1, source_target_pairs={{8,0},{16,8},{24,16},{32,24},{40,32},{48,40},{56,48},{64,56},{72,6... | collective-permute-start | bytes 3145736 | tf_op jit(solution)/shard_map/ppermute | solution.py:394
  15.8 2.5 %collective-permute-start.2 = (f32[2,256,256]{2,1,0:T(8,128)S(1)}, f32[2,256,256]{2,1,0:T(8,128)S(1)}, u32[]{:S(2)}, u32[]{:S(2)}) collective-permute-start(f32[2,256,256]{2,1,0:T(8,128)S(1)} %slice.11), channel_id=1, source_target_pairs={{9,0},{10,1},{11,2},{12,3},{13,4},{14,5},{15,6},{17,8},{18,9},{19,... | collective-permute-start | bytes 1572872 | tf_op jit(solution)/shard_map/ppermute | solution.py:404
  18.3 12.0 %collective-permute-done.refs_8_.refs_9_ = f32[2,512,256]{2,1,0:T(8,128)S(1)} collective-permute-done((f32[2,512,256]{2,1,0:T(8,128)S(1)}, f32[2,512,256]{2,1,0:T(8,128)S(1)}, u32[]{:S(2)}, u32[]{:S(2)}) %collective-permute-start) | collective-permute-done | bytes 1048608 | tf_op jit(solution)/shard_map/ppermute | solution.py:394
  30.3 0.0 copy-start.7
  30.3 1.0 copy-done.7
  31.3 7.0 %shard_map.123 = (f32[2,256,256]{2,1,0:T(8,128)}, f32[2,256,256]{2,1,0:T(8,128)}, f32[2,4,256,128]{3,2,1,0:T(8,128)}, f32[2,2,256,128]{3,2,1,0:T(8,128)}) custom-call(s32[1]{0:T(128)S(6)} %copy.13.refs_0_, s32[2,16]{1,0:T(2,128)} %bitcast.11, f32[2,256,256]{2,1,0:T(8,128)} %probe.1, f32[2,2,256,128]{3,2,1,0:T(8,128)} %get-tuple-element.31.refs_3_, ...), custom_call_target="tpu_custom_call" | custom-call | flops 1048576 | bytes 1048576 | tf_op jit(solution)/shard_map/pallas_call | solution.py:358
  38.3 6.9 %collective-permute-done.2.refs_10_ = f32[2,256,256]{2,1,0:T(8,128)S(1)} collective-permute-done((f32[2,256,256]{2,1,0:T(8,128)S(1)}, f32[2,256,256]{2,1,0:T(8,128)S(1)}, u32[]{:S(2)}, u32[]{:S(2)}) %collective-permute-start.2) | collective-permute-done | bytes 524320 | tf_op jit(solution)/shard_map/ppermute | solution.py:404
  45.2 0.0 copy-start.9
  45.2 3.6 %collective-permute-done.1.refs_8_ = f32[2,256,512]{2,1,0:T(8,128)S(1)} collective-permute-done((f32[2,256,512]{2,1,0:T(8,128)S(1)}, f32[2,256,512]{2,1,0:T(8,128)S(1)}, u32[]{:S(2)}, u32[]{:S(2)}) %collective-permute-start.1) | collective-permute-done | bytes 1048608 | tf_op jit(solution)/shard_map/ppermute | solution.py:394
  48.8 0.0 copy-start.8
  48.8 4.4 %collective-permute-start.3 = (f32[2,256,256]{2,1,0:T(8,128)}, f32[2,256,256]{2,1,0:T(8,128)S(1)}, u32[]{:S(2)}, u32[]{:S(2)}) collective-permute-start(f32[2,256,256]{2,1,0:T(8,128)} %get-tuple-element.45), channel_id=1, source_target_pairs={{0,1},{1,2},{2,3},{3,4},{4,5},{5,6},{6,7},{8,9},{9,10},{10,11},{11... | collective-permute-start | bytes 1572872 | tf_op jit(solution)/shard_map/ppermute | solution.py:394
  53.2 0.0 copy-done.9
  53.2 0.0 copy-done.8
  53.2 7.8 %shard_map.124 = (f32[2,256,256]{2,1,0:T(8,128)}, f32[2,256,256]{2,1,0:T(8,128)}, f32[2,256,256]{2,1,0:T(8,128)}, f32[2,256,256]{2,1,0:T(8,128)}, f32[2,256,512]{2,1,0:T(8,128)}, /*index=5*/f32[2,2,256,128]{3,2,1,0:T(8,128)}) custom-call(s32[1]{0:T(128)S(6)} %copy.13.refs_0_, s32[2,16]{1,0:T(2,128)} %bitcast.12, f32[2,256,256]{2,1,0:T(8,128)} %probe.1, ...), custom_call_target="tpu_custom_call" | custom-call | flops 1048576 | bytes 1048576 | tf_op jit(solution)/shard_map/pallas_call | solution.py:358
  61.1 0.0 copy-start.1
  61.1 0.0 copy-start.2
  61.1 2.5 %collective-permute-done.3.left_top = f32[2,256,256]{2,1,0:T(8,128)S(1)} collective-permute-done((f32[2,256,256]{2,1,0:T(8,128)}, f32[2,256,256]{2,1,0:T(8,128)S(1)}, u32[]{:S(2)}, u32[]{:S(2)}) %collective-permute-start.3) | collective-permute-done | bytes 524320 | tf_op jit(solution)/shard_map/ppermute | solution.py:394
  63.6 0.0 copy-start.5
  63.6 0.8 copy-done.5
  64.4 14.1 %all-to-all-start = ((f32[128,8,128]{2,1,0:T(8,128)}), f32[128,8,128]{2,1,0:T(8,128)}, u32[]{:S(2)}, u32[]{:S(2)}) async-start(f32[128,8,128]{2,1,0:T(8,128)} %bitcast.8), calls=%async_computation | async-start | bytes 1048576 | tf_op jit(solution)/shard_map/all_to_all | solution.py:446
  78.5 7.5 %collective-permute-start.4 = (f32[2,256,256]{2,1,0:T(8,128)}, f32[2,256,256]{2,1,0:T(8,128)}, u32[]{:S(2)}, u32[]{:S(2)}) collective-permute-start(f32[2,256,256]{2,1,0:T(8,128)} %get-tuple-element.49), channel_id=1, source_target_pairs={{0,9},{1,10},{2,11},{3,12},{4,13},{5,14},{6,15},{8,17},{9,18},{10,... | collective-permute-start | bytes 1572872 | tf_op jit(solution)/shard_map/ppermute | solution.py:404
  86.0 3.9 %all-to-all-done = f32[128,8,128]{2,1,0:T(8,128)} async-done(((f32[128,8,128]{2,1,0:T(8,128)}), f32[128,8,128]{2,1,0:T(8,128)}, u32[]{:S(2)}, u32[]{:S(2)}) %all-to-all-start) | async-done | bytes 524320 | tf_op jit(solution)/shard_map/all_to_all | solution.py:446
  89.9 1.1 reduce_sum.18
  91.0 0.6 broadcast_in_dim.7
  91.6 11.0 %all-to-all-start.1 = ((f32[16,8,128]{2,1,0:T(8,128)}), f32[16,8,128]{2,1,0:T(8,128)S(1)}, u32[]{:S(2)}, u32[]{:S(2)}) async-start(f32[16,8,128]{2,1,0:T(8,128)} %bitcast.3), calls=%async_computation.1 | async-start | bytes 131072 | tf_op jit(solution)/shard_map/all_to_all | solution.py:450
  102.7 3.6 %collective-permute-start.6 = (f32[2,256,256]{2,1,0:T(8,128)}, f32[2,256,256]{2,1,0:T(8,128)}, u32[]{:S(2)}, u32[]{:S(2)}) collective-permute-start(f32[2,256,256]{2,1,0:T(8,128)} %get-tuple-element.52), channel_id=1, source_target_pairs={{0,8},{8,16},{16,24},{24,32},{32,40},{40,48},{48,56},{56,64},{64,7... | collective-permute-start | bytes 1572872 | tf_op jit(solution)/shard_map/ppermute | solution.py:394
  106.3 1.9 %collective-permute-start.7 = (f32[2,256,256]{2,1,0:T(8,128)}, f32[2,256,256]{2,1,0:T(8,128)}, u32[]{:S(2)}, u32[]{:S(2)}) collective-permute-start(f32[2,256,256]{2,1,0:T(8,128)} %get-tuple-element.53), channel_id=1, source_target_pairs={{0,8},{8,16},{16,24},{24,32},{32,40},{40,48},{48,56},{56,64},{64,7... | collective-permute-start | bytes 1572872 | tf_op jit(solution)/shard_map/ppermute | solution.py:394
  108.2 0.0 all-to-all-done.1
  108.3 0.0 collective-permute-done.4.across
  108.3 1.9 %collective-permute-start.5 = (f32[2,256,256]{2,1,0:T(8,128)}, f32[2,256,256]{2,1,0:T(8,128)}, u32[]{:S(2)}, u32[]{:S(2)}) collective-permute-start(f32[2,256,256]{2,1,0:T(8,128)} %get-tuple-element.51), channel_id=1, source_target_pairs={{0,1},{1,2},{2,3},{3,4},{4,5},{5,6},{6,7},{8,9},{9,10},{10,11},{11... | collective-permute-start | bytes 1572872 | tf_op jit(solution)/shard_map/ppermute | solution.py:394
  110.2 0.9 broadcast_in_dim.8
  111.1 7.0 %all-to-all-start.2 = ((f32[128,8,128]{2,1,0:T(8,128)}), f32[128,8,128]{2,1,0:T(8,128)}, u32[]{:S(2)}, u32[]{:S(2)}) async-start(f32[128,8,128]{2,1,0:T(8,128)} %bitcast.7), calls=%async_computation.2 | async-start | bytes 1048576 | tf_op jit(solution)/shard_map/all_to_all | solution.py:454
  118.1 0.0 collective-permute-done.6.above_left
  118.1 0.3 collective-permute-done.7.above_right
  118.3 12.3 %collective-permute-done.5.left_low = f32[2,256,256]{2,1,0:T(8,128)} collective-permute-done((f32[2,256,256]{2,1,0:T(8,128)}, f32[2,256,256]{2,1,0:T(8,128)}, u32[]{:S(2)}, u32[]{:S(2)}) %collective-permute-start.5) | collective-permute-done | bytes 524320 | tf_op jit(solution)/shard_map/ppermute | solution.py:394
  130.6 0.0 copy-done.1
  130.6 0.0 copy-done.2
  130.6 0.0 copy-start.3
  130.6 1.0 copy-done.3
  131.6 0.0 copy-start.4
  131.7 1.0 copy-done.4
  132.7 0.0 copy-start.6
  132.7 1.0 copy-done.6
  133.7 3.2 %shard_map.125 = f32[2,512,512]{2,1,0:T(8,128)} custom-call(f32[2,512,512]{2,1,0:T(8,128)S(1)} %copy-done.1, f32[2,256,256]{2,1,0:T(8,128)S(1)} %copy-done.3, f32[2,256,256]{2,1,0:T(8,128)S(1)} %copy-done.4, f32[2,256,512]{2,1,0:T(8,128)S(1)} %copy-done.2, f32[2,256,256]{2,1,0:T(8,128)S(1)} %copy-done.6, f32[2,256,256]{2,1,0:T(8,128)} %collective-permute-done.5.left_low, ...), custom_call_target="tpu_custom_call" | custom-call | flops 1048576 | bytes 1048576 | tf_op jit(solution)/shard_map/pallas_call | solution.py:420
  136.9 0.0 all-to-all-done.2
  136.9 2.1 %shard_map.126 = f32[2,256,256]{2,1,0:T(8,128)} custom-call(f32[2,256,256]{2,1,0:T(8,128)} %probe.1, f32[2,2,256,128]{3,2,1,0:T(8,128)} %bitcast.6.total), custom_call_target="tpu_custom_call" | custom-call | flops 1048576 | bytes 1048576 | tf_op jit(solution)/shard_map/pallas_call | solution.py:436
  (2 shorter events, 0.0 us)
Async XLA Ops:
  1.9 28.4 %collective-permute-start = (f32[2,512,256]{2,1,0:T(8,128)S(1)}, f32[2,512,256]{2,1,0:T(8,128)S(1)}, u32[]{:S(2)}, u32[]{:S(2)}) collective-permute-start(f32[2,512,256]{2,1,0:T(8,128)S(1)} %slice.9), channel_id=1, source_target_pairs={{1,0},{2,1},{3,2},{4,3},{5,4},{6,5},{7,6},{9,8},{10,9},{11,10},{12... | collective-permute-start | bytes 3145736 | tf_op jit(solution)/shard_map/ppermute | solution.py:394
  6.0 4.7 %copy-start = (f32[2,512,512]{2,1,0:T(8,128)S(1)}, f32[2,512,512]{2,1,0:T(8,128)}, u32[]{:S(2)}) copy-start(f32[2,512,512]{2,1,0:T(8,128)} %tile.1) | copy-start | bytes 6291460
  10.9 38.0 %collective-permute-start.1 = (f32[2,256,512]{2,1,0:T(8,128)S(1)}, f32[2,256,512]{2,1,0:T(8,128)S(1)}, u32[]{:S(2)}, u32[]{:S(2)}) collective-permute-start(f32[2,256,512]{2,1,0:T(8,128)S(1)} %slice.10), channel_id=1, source_target_pairs={{8,0},{16,8},{24,16},{32,24},{40,32},{48,40},{56,48},{64,56},{72,6... | collective-permute-start | bytes 3145736 | tf_op jit(solution)/shard_map/ppermute | solution.py:394
  15.8 29.4 %collective-permute-start.2 = (f32[2,256,256]{2,1,0:T(8,128)S(1)}, f32[2,256,256]{2,1,0:T(8,128)S(1)}, u32[]{:S(2)}, u32[]{:S(2)}) collective-permute-start(f32[2,256,256]{2,1,0:T(8,128)S(1)} %slice.11), channel_id=1, source_target_pairs={{9,0},{10,1},{11,2},{12,3},{13,4},{14,5},{15,6},{17,8},{18,9},{19,... | collective-permute-start | bytes 1572872 | tf_op jit(solution)/shard_map/ppermute | solution.py:404
  30.3 1.0 copy-start.7
  45.2 8.0 %copy-start.9 = (f32[2,256,256]{2,1,0:T(8,128)}, f32[2,256,256]{2,1,0:T(8,128)S(1)}, u32[]{:S(2)}) copy-start(f32[2,256,256]{2,1,0:T(8,128)S(1)} %collective-permute-done.2.refs_10_) | copy-start | bytes 1572868
  48.8 4.4 %copy-start.8 = (f32[2,256,512]{2,1,0:T(8,128)}, f32[2,256,512]{2,1,0:T(8,128)S(1)}, u32[]{:S(2)}) copy-start(f32[2,256,512]{2,1,0:T(8,128)S(1)} %collective-permute-done.1.refs_8_) | copy-start | bytes 3145732
  48.8 14.8 %collective-permute-start.3 = (f32[2,256,256]{2,1,0:T(8,128)}, f32[2,256,256]{2,1,0:T(8,128)S(1)}, u32[]{:S(2)}, u32[]{:S(2)}) collective-permute-start(f32[2,256,256]{2,1,0:T(8,128)} %get-tuple-element.45), channel_id=1, source_target_pairs={{0,1},{1,2},{2,3},{3,4},{4,5},{5,6},{6,7},{8,9},{9,10},{10,11},{11... | collective-permute-start | bytes 1572872 | tf_op jit(solution)/shard_map/ppermute | solution.py:394
  61.1 69.5 %copy-start.1 = (f32[2,512,512]{2,1,0:T(8,128)S(1)}, f32[2,512,512]{2,1,0:T(8,128)}, u32[]{:S(2)}) copy-start(f32[2,512,512]{2,1,0:T(8,128)} %tile.1) | copy-start | bytes 6291460
  61.1 69.5 %copy-start.2 = (f32[2,256,512]{2,1,0:T(8,128)S(1)}, f32[2,256,512]{2,1,0:T(8,128)}, u32[]{:S(2)}) copy-start(f32[2,256,512]{2,1,0:T(8,128)} %get-tuple-element.44.lower) | copy-start | bytes 3145732
  63.6 0.8 copy-start.5
  64.4 25.5 %all-to-all-start = ((f32[128,8,128]{2,1,0:T(8,128)}), f32[128,8,128]{2,1,0:T(8,128)}, u32[]{:S(2)}, u32[]{:S(2)}) async-start(f32[128,8,128]{2,1,0:T(8,128)} %bitcast.8), calls=%async_computation | async-start | bytes 1048576 | tf_op jit(solution)/shard_map/all_to_all | solution.py:446
  78.5 29.8 %collective-permute-start.4 = (f32[2,256,256]{2,1,0:T(8,128)}, f32[2,256,256]{2,1,0:T(8,128)}, u32[]{:S(2)}, u32[]{:S(2)}) collective-permute-start(f32[2,256,256]{2,1,0:T(8,128)} %get-tuple-element.49), channel_id=1, source_target_pairs={{0,9},{1,10},{2,11},{3,12},{4,13},{5,14},{6,15},{8,17},{9,18},{10,... | collective-permute-start | bytes 1572872 | tf_op jit(solution)/shard_map/ppermute | solution.py:404
  91.6 16.6 %all-to-all-start.1 = ((f32[16,8,128]{2,1,0:T(8,128)}), f32[16,8,128]{2,1,0:T(8,128)S(1)}, u32[]{:S(2)}, u32[]{:S(2)}) async-start(f32[16,8,128]{2,1,0:T(8,128)} %bitcast.3), calls=%async_computation.1 | async-start | bytes 131072 | tf_op jit(solution)/shard_map/all_to_all | solution.py:450
  102.7 15.4 %collective-permute-start.6 = (f32[2,256,256]{2,1,0:T(8,128)}, f32[2,256,256]{2,1,0:T(8,128)}, u32[]{:S(2)}, u32[]{:S(2)}) collective-permute-start(f32[2,256,256]{2,1,0:T(8,128)} %get-tuple-element.52), channel_id=1, source_target_pairs={{0,8},{8,16},{16,24},{24,32},{32,40},{40,48},{48,56},{56,64},{64,7... | collective-permute-start | bytes 1572872 | tf_op jit(solution)/shard_map/ppermute | solution.py:394
  106.3 12.0 %collective-permute-start.7 = (f32[2,256,256]{2,1,0:T(8,128)}, f32[2,256,256]{2,1,0:T(8,128)}, u32[]{:S(2)}, u32[]{:S(2)}) collective-permute-start(f32[2,256,256]{2,1,0:T(8,128)} %get-tuple-element.53), channel_id=1, source_target_pairs={{0,8},{8,16},{16,24},{24,32},{32,40},{40,48},{48,56},{56,64},{64,7... | collective-permute-start | bytes 1572872 | tf_op jit(solution)/shard_map/ppermute | solution.py:394
  108.3 22.3 %collective-permute-start.5 = (f32[2,256,256]{2,1,0:T(8,128)}, f32[2,256,256]{2,1,0:T(8,128)}, u32[]{:S(2)}, u32[]{:S(2)}) collective-permute-start(f32[2,256,256]{2,1,0:T(8,128)} %get-tuple-element.51), channel_id=1, source_target_pairs={{0,1},{1,2},{2,3},{3,4},{4,5},{5,6},{6,7},{8,9},{9,10},{10,11},{11... | collective-permute-start | bytes 1572872 | tf_op jit(solution)/shard_map/ppermute | solution.py:394
  111.1 25.8 %all-to-all-start.2 = ((f32[128,8,128]{2,1,0:T(8,128)}), f32[128,8,128]{2,1,0:T(8,128)}, u32[]{:S(2)}, u32[]{:S(2)}) async-start(f32[128,8,128]{2,1,0:T(8,128)} %bitcast.7), calls=%async_computation.2 | async-start | bytes 1048576 | tf_op jit(solution)/shard_map/all_to_all | solution.py:454
  130.6 1.0 copy-start.3
  131.6 1.0 copy-start.4
  132.7 1.0 copy-start.6

commit v4 on v3

--- a/solution.py
+++ b/solution.py
@@ -305,6 +305,9 @@
         if kind == "grad":
             pairs = [(grad.at[:, pl.ds(panel, panels), pl.ds(row, out.shape[2]), :], out)]
         else:
+            here = pl.ds(panel, panels), pl.ds(row, out.shape[1])
+            if kind == "tile":
+                grad[:, *here, :] = ext[:, *here, :] - 0.25 * grad[:, *here, :]
             pairs = []
             for part in range(2):
                 first = out.shape[2] // HALF - panels
@@ -325,14 +328,14 @@
     "base": 0, "panels": 5, "keep": (0, SIDE, 0, SIDE), "first": True,
     "in": [("ext", 0, 0, 4, 0, TILE)],
     "zero": [(0, 4, 0, TILE)],
-    "out": [("array", 0, 0, 2), ("grad", 0, SIDE, 2), ("grad", 2, 0, 2)],
+    "out": [("tile", 0, 0, 2), ("grad", 0, SIDE, 2), ("grad", 2, 0, 2)],
     "shapes": [(2, SIDE, SIDE), (2, 2, SIDE, HALF), (2, 2, TILE, HALF)],
 }
 PLAN_RIGHT = {
     "base": 2, "panels": 4, "keep": (0, SIDE, SIDE + 1, TILE), "first": False,
     "in": [("ext", 0, 0, 2, 0, TILE), ("ext", 2, 0, 2, 0, TILE), ("grad", 0, 0, 2, 0, TILE)],
     "zero": [(2, 2, 0, TILE)],
-    "out": [("array", 0, 0, 2), ("array", 2, 0, 2), ("grad", 0, SIDE, 4)],
+    "out": [("tile", 0, 0, 2), ("array", 2, 0, 2), ("grad", 0, SIDE, 4)],
     "shapes": [(2, SIDE, SIDE), (2, SIDE, SIDE), (2, 4, SIDE, HALF)],
 }
 PLAN_LOWER = {
@@ -343,7 +346,7 @@
     ],
     "zero": [(0, 6, TILE, SIDE)],
     "out": [
-        ("array", 4, TILE, 2), ("array", 4, SIDE, 2), ("array", 0, TILE, 2), ("array", 2, TILE, 2), ("array", 0, SIDE, 4),
+        ("array", 4, TILE, 2), ("array", 4, SIDE, 2), ("array", 0, TILE, 2), ("array", 2, TILE, 2), ("tile", 0, SIDE, 4),
     ],
     "shapes": [(2, SIDE, SIDE), (2, SIDE, SIDE), (2, SIDE, SIDE), (2, SIDE, SIDE), (2, SIDE, TILE)],
 }
@@ -404,40 +407,79 @@
     return lax.ppermute(block, ROW_AXES + COL_AXES, pairs)
 
 
-def update_kernel(tile, top_left, top_right, lower, left_top, left_low, above_left, above_right, across, out):
+def copied(pairs, sems):
+    copies = [pltpu.make_async_copy(*pair, sems.at[i]) for i, pair in enumerate(pairs)]
+    for copy in copies:
+        copy.start()
+    for copy in copies:
+        copy.wait()
+
+
+def top_kernel(
+    top_left, top_right, lower, left_top, above_left, above_right, across, out,
+    tile_v, left_v, above_v, across_v, sems,
+):
     top, low = pl.ds(0, SIDE), pl.ds(SIDE, TILE - SIDE)
     first, second = pl.ds(0, SIDE), pl.ds(SIDE, TILE - SIDE)
+    copied([
+        (top_left, tile_v.at[:, top, first]), (top_right, tile_v.at[:, top, second]), (lower, tile_v.at[:, low, :]),
+        (above_left, above_v.at[0]), (above_right, above_v.at[1]), (across, across_v), (left_top, left_v),
+    ], sems)
     for part in range(2):
-        out[part, top, first] = tile[part, top, first] - 0.25 * (
-            (top_left[part] + left_top[part]) + (above_left[part] + across[part])
-        )
-        out[part, top, second] = tile[part, top, second] - 0.25 * (top_right[part] + above_right[part])
-        out[part, low, first] = tile[part, low, first] - 0.25 * (lower[part, :, first] + left_low[part])
-        out[part, low, second] = tile[part, low, second] - 0.25 * lower[part, :, second]
-
-
-def update(tile, *parts):
-    return pl.pallas_call(
-        update_kernel,
-        out_shape=jax.ShapeDtypeStruct(tile.shape, F32),
-        compiler_params=pltpu.CompilerParams(vmem_limit_bytes=32 * 1024 * 1024),
-        cost_estimate=pl.CostEstimate(flops=2**20, bytes_accessed=2**20, transcendentals=0),
-    )(tile, *parts)
-
-
-def probe_kernel(scale, probe, total, out):
+        tile_v[part, top, first] -= 0.25 * (left_v[part] + (above_v[0, part] + across_v[part]))
+        tile_v[part, top, second] -= 0.25 * above_v[1, part]
+    copied([(tile_v.at[part], out.at[part]) for part in range(2)], sems)
+
+
+def low_kernel(scale, tile, left_low, probe, total, out, probe_out, tile_v, left_v, probe_v, total_v, sems):
+    corner = pl.ds(0, 2), pl.ds(SIDE, TILE - SIDE), pl.ds(0, SIDE)
+    copied([(tile.at[corner], tile_v), (left_low, left_v), (probe, probe_v), (total, total_v)], sems)
+    tile_v[...] -= 0.25 * left_v[...]
     for part in range(2):
         for h in range(2):
             cols = pl.ds(h * HALF, HALF)
-            out[part, :, cols] = probe[part, :, cols] - scale * total[part, h]
-
-
-def probe_update(scale, probe, total):
+            probe_v[part, :, cols] -= scale * total_v[part, h]
+    copied([(tile_v, out.at[corner]), (probe_v, probe_out)], sems)
+
+
+def update_top(*parts):
+    any_spec = pl.BlockSpec(memory_space=pl.ANY)
     return pl.pallas_call(
-        functools.partial(probe_kernel, scale),
-        out_shape=jax.ShapeDtypeStruct(probe.shape, F32),
+        top_kernel,
+        out_shape=jax.ShapeDtypeStruct((2, TILE, TILE), F32),
+        in_specs=[any_spec] * len(parts),
+        out_specs=any_spec,
+        scratch_shapes=[
+            pltpu.VMEM((2, TILE, TILE), F32),
+            pltpu.VMEM((2, SIDE, SIDE), F32),
+            pltpu.VMEM((2, 2, SIDE, SIDE), F32),
+            pltpu.VMEM((2, SIDE, SIDE), F32),
+            pltpu.SemaphoreType.DMA((7,)),
+        ],
+        compiler_params=pltpu.CompilerParams(vmem_limit_bytes=56 * 1024 * 1024),
         cost_estimate=pl.CostEstimate(flops=2**20, bytes_accessed=2**20, transcendentals=0),
-    )(probe, total)
+    )(*parts)
+
+
+def update_low(scale, *parts):
+    any_spec = pl.BlockSpec(memory_space=pl.ANY)
+    tile, left_low, probe, total = parts
+    return pl.pallas_call(
+        functools.partial(low_kernel, scale),
+        out_shape=[jax.ShapeDtypeStruct(tile.shape, F32), jax.ShapeDtypeStruct(probe.shape, F32)],
+        in_specs=[any_spec] * len(parts),
+        out_specs=[any_spec] * 2,
+        scratch_shapes=[
+            pltpu.VMEM(left_low.shape, F32),
+            pltpu.VMEM(left_low.shape, F32),
+            pltpu.VMEM(probe.shape, F32),
+            pltpu.VMEM(total.shape, F32),
+            pltpu.SemaphoreType.DMA((4,)),
+        ],
+        input_output_aliases={0: 0},
+        compiler_params=pltpu.CompilerParams(vmem_limit_bytes=56 * 1024 * 1024),
+        cost_estimate=pl.CostEstimate(flops=2**20, bytes_accessed=2**20, transcendentals=0),
+    )(*parts)
 
 
 def total_over_all(x, before):
@@ -479,13 +521,10 @@
     above_left = passed_along(below_left, ROW_AXES, 1)
     above_right = passed_along(below_right, ROW_AXES, 1)
     left_top, probe_grad = lax.optimization_barrier((left_top, probe_grad))
-    total_grad, (from_across, right_low) = total_over_all(probe_grad, (from_across, right_low))
+    total_grad, (from_across, above_left, right_low) = total_over_all(probe_grad, (from_across, above_left, right_low))
     left_low = passed_along(right_low, COL_AXES, 1)
-    object_next = update(
-        object_field, top_left, top_right, lower, left_top, left_low, above_left, above_right, from_across
-    )
-    object_next, total_grad = lax.optimization_barrier((object_next, total_grad))
-    probe_next = probe_update(1.0 / math.sqrt(positions), probe, total_grad)
+    tile = update_top(top_left, top_right, lower, left_top, above_left, above_right, from_across)
+    object_next, probe_next = update_low(1.0 / math.sqrt(positions), tile, left_low, probe, total_grad)
     return (object_next, probe_next)
 
 

time: 139 us -> 133 us (0.957); the launches traced: 139 us -> 130 us
  Pallas kernels: 24.7 us -> 45.8 us
  starting transfers between devices: 61.8 us -> 45 us
  waiting for transfers between devices: 41.5 us -> 31.4 us
  local copies, waits for them, and re-layouts: 8.41 us -> 6.24 us
    ppermute x6, waiting for transfers between devices: 30.6 us -> 9.1 us  [passed_along(): return lax.ppermute(block, axes, route)]
    pallas_call x3, Pallas kernels: 19.5 us -> 39.5 us  [slots_call(): pl.pallas_call(functools.partial(slots_kernel, plan), out_shape=[jax.Shap...]
    all_to_all x1, waiting for transfers between devices: 0.01 us -> 9.64 us  [total_over_all(): lax.all_to_all(copies, NEAR_AXES, 0, 0, tiled=True).reshape(x.shape)]
    all_to_all x1, starting transfers between devices: 11 us -> 3.94 us  [total_over_all(): share = lax.all_to_all(copies, FAR_AXES, 0, 0, tiled=True)]
    all_to_all x1, starting transfers between devices: 14.1 us -> 7.5 us  [total_over_all(): shares = lax.all_to_all(blocks, NEAR_AXES, 0, 0, tiled=True)]
    ppermute x2, starting transfers between devices: 10.1 us -> 6.14 us  [passed_across(): return lax.ppermute(block, ROW_AXES + COL_AXES, pairs)]
    all_to_all x1, waiting for transfers between devices: 3.89 us -> 7.38 us  [total_over_all(): shares = lax.all_to_all(blocks, NEAR_AXES, 0, 0, tiled=True)]
    unnamed x20, local copies, waits for them, and re-layouts: 4.91 us -> 2.74 us
  transfers between devices with their start and end apart: 11 -> 11, of which waited for: 7 -> 5; matrix products, arithmetic and copies ran while one was open for 2% -> 2% of each run, Pallas kernels for 16% -> 33%
where the time goes in v4:
time: 133 us; the launch traced here: 130 us
  Pallas kernels  45.8 us (34%)
  starting transfers between devices  45 us (34%)
  waiting for transfers between devices  31.4 us (24%)
  local copies, waits for them, and re-layouts  6.24 us (5%)
  between operations  1.54 us (1%)
    pallas_call x3, Pallas kernels, slots_call(): pl.pallas_call(functools.partial(slots_kernel, plan), out_shape=[jax.Shap...  39.5 us
    ppermute x6, starting transfers between devices, passed_along(): return lax.ppermute(block, axes, route)  20.3 us
    all_to_all x1, waiting for transfers between devices, total_over_all(): lax.all_to_all(copies, NEAR_AXES, 0, 0, tiled=True).reshape(x.shape)  9.64 us
    ppermute x6, waiting for transfers between devices, passed_along(): return lax.ppermute(block, axes, route)  9.1 us
    all_to_all x1, starting transfers between devices, total_over_all(): shares = lax.all_to_all(blocks, NEAR_AXES, 0, 0, tiled=True)  7.5 us
    all_to_all x1, waiting for transfers between devices, total_over_all(): shares = lax.all_to_all(blocks, NEAR_AXES, 0, 0, tiled=True)  7.38 us
    all_to_all x1, starting transfers between devices, total_over_all(): lax.all_to_all(copies, NEAR_AXES, 0, 0, tiled=True).reshape(x.shape)  7.18 us
    ppermute x2, starting transfers between devices, passed_across(): return lax.ppermute(block, ROW_AXES + COL_AXES, pairs)  6.14 us
  transfers between devices with their start and end apart: 11, of which 5 were waited for; matrix products, arithmetic and copies ran while one was open for 2% of the time, Pallas kernels for 33%

profile of v4, /device:TPU:25, one launch (start us, length us, event | category | flops | bytes accessed | tf_op | source)
XLA Modules:
  0.0 130.1 jit_solution(13048431607124598431)
XLA Ops:
  0.6 1.3 slice.9
  1.9 2.9 %collective-permute-start = (f32[2,512,256]{2,1,0:T(8,128)S(1)}, f32[2,512,256]{2,1,0:T(8,128)S(1)}, u32[]{:S(2)}, u32[]{:S(2)}) collective-permute-start(f32[2,512,256]{2,1,0:T(8,128)S(1)} %slice.9), channel_id=1, source_target_pairs={{1,0},{2,1},{3,2},{4,3},{5,4},{6,5},{7,6},{9,8},{10,9},{11,10},{12... | collective-permute-start | bytes 3145736 | tf_op jit(solution)/shard_map/ppermute | solution.py:397
  5.4 0.6 broadcast_in_dim.6.refs_3_
  6.0 0.0 copy-start
  6.1 11.6 %shard_map.122 = (f32[2,256,256]{2,1,0:T(8,128)}, f32[2,2,256,128]{3,2,1,0:T(8,128)}, f32[2,2,512,128]{3,2,1,0:T(8,128)}, f32[2,2,256,128]{3,2,1,0:T(8,128)}) custom-call(s32[1]{0:T(128)S(6)} %copy.15.refs_0_, s32[2,16]{1,0:T(2,128)} %bitcast.11, f32[2,256,256]{2,1,0:T(8,128)} %probe.1, f32[2,2,8,128]{3,2,1,0:T(8,128)} %broadcast_in_dim.6.refs_3_, ...), custom_call_target="tpu_custom_call" | custom-call | flops 1048576 | bytes 1048576 | tf_op jit(solution)/shard_map/pallas_call | solution.py:361
  17.7 0.0 copy-done
  17.7 0.1 slice.10
  17.8 2.8 %collective-permute-start.1 = (f32[2,256,512]{2,1,0:T(8,128)S(1)}, f32[2,256,512]{2,1,0:T(8,128)S(1)}, u32[]{:S(2)}, u32[]{:S(2)}) collective-permute-start(f32[2,256,512]{2,1,0:T(8,128)S(1)} %slice.10), channel_id=1, source_target_pairs={{8,0},{16,8},{24,16},{32,24},{40,32},{48,40},{56,48},{64,56},{72,6... | collective-permute-start | bytes 3145736 | tf_op jit(solution)/shard_map/ppermute | solution.py:397
  20.6 4.2 %collective-permute-start.2 = (f32[2,256,256]{2,1,0:T(8,128)S(1)}, f32[2,256,256]{2,1,0:T(8,128)S(1)}, u32[]{:S(2)}, u32[]{:S(2)}) collective-permute-start(f32[2,256,256]{2,1,0:T(8,128)S(1)} %slice.11), channel_id=1, source_target_pairs={{9,0},{10,1},{11,2},{12,3},{13,4},{14,5},{15,6},{17,8},{18,9},{19,... | collective-permute-start | bytes 1572872 | tf_op jit(solution)/shard_map/ppermute | solution.py:407
  24.8 5.5 %collective-permute-done.refs_8_.refs_9_ = f32[2,512,256]{2,1,0:T(8,128)S(1)} collective-permute-done((f32[2,512,256]{2,1,0:T(8,128)S(1)}, f32[2,512,256]{2,1,0:T(8,128)S(1)}, u32[]{:S(2)}, u32[]{:S(2)}) %collective-permute-start) | collective-permute-done | bytes 1048608 | tf_op jit(solution)/shard_map/ppermute | solution.py:397
  30.3 0.0 copy-start.1
  30.3 1.0 copy-done.1
  31.3 8.6 %shard_map.123 = (f32[2,256,256]{2,1,0:T(8,128)}, f32[2,256,256]{2,1,0:T(8,128)}, f32[2,4,256,128]{3,2,1,0:T(8,128)}, f32[2,2,256,128]{3,2,1,0:T(8,128)}) custom-call(s32[1]{0:T(128)S(6)} %copy.15.refs_0_, s32[2,16]{1,0:T(2,128)} %bitcast.12, f32[2,256,256]{2,1,0:T(8,128)} %probe.1, f32[2,2,256,128]{3,2,1,0:T(8,128)} %get-tuple-element.30.refs_3_, ...), custom_call_target="tpu_custom_call" | custom-call | flops 1048576 | bytes 1048576 | tf_op jit(solution)/shard_map/pallas_call | solution.py:361
  39.9 5.3 %collective-permute-done.2.refs_10_ = f32[2,256,256]{2,1,0:T(8,128)S(1)} collective-permute-done((f32[2,256,256]{2,1,0:T(8,128)S(1)}, f32[2,256,256]{2,1,0:T(8,128)S(1)}, u32[]{:S(2)}, u32[]{:S(2)}) %collective-permute-start.2) | collective-permute-done | bytes 524320 | tf_op jit(solution)/shard_map/ppermute | solution.py:407
  45.2 0.0 copy-start.8
  45.2 3.6 %collective-permute-done.1.refs_8_ = f32[2,256,512]{2,1,0:T(8,128)S(1)} collective-permute-done((f32[2,256,512]{2,1,0:T(8,128)S(1)}, f32[2,256,512]{2,1,0:T(8,128)S(1)}, u32[]{:S(2)}, u32[]{:S(2)}) %collective-permute-start.1) | collective-permute-done | bytes 1048608 | tf_op jit(solution)/shard_map/ppermute | solution.py:397
  48.8 0.0 copy-start.3
  48.8 5.0 %collective-permute-start.3 = (f32[2,256,256]{2,1,0:T(8,128)}, f32[2,256,256]{2,1,0:T(8,128)S(1)}, u32[]{:S(2)}, u32[]{:S(2)}) collective-permute-start(f32[2,256,256]{2,1,0:T(8,128)} %get-tuple-element.44), channel_id=1, source_target_pairs={{0,1},{1,2},{2,3},{3,4},{4,5},{5,6},{6,7},{8,9},{9,10},{10,11},{11... | collective-permute-start | bytes 1572872 | tf_op jit(solution)/shard_map/ppermute | solution.py:397
  53.8 0.0 copy-done.8
  53.8 0.0 copy-done.3
  53.8 19.2 %shard_map.124 = (f32[2,256,256]{2,1,0:T(8,128)}, f32[2,256,256]{2,1,0:T(8,128)}, f32[2,256,256]{2,1,0:T(8,128)}, f32[2,256,256]{2,1,0:T(8,128)}, f32[2,256,512]{2,1,0:T(8,128)}, /*index=5*/f32[2,2,256,128]{3,2,1,0:T(8,128)}) custom-call(s32[1]{0:T(128)S(6)} %copy.15.refs_0_, s32[2,16]{1,0:T(2,128)} %bitcast.13, f32[2,256,256]{2,1,0:T(8,128)} %probe.1, ...), custom_call_target="tpu_custom_call" | custom-call | flops 1048576 | bytes 1048576 | tf_op jit(solution)/shard_map/pallas_call | solution.py:361
  73.1 0.0 collective-permute-done.3.left_top
  73.1 0.0 copy-start.4
  73.1 7.5 %all-to-all-start = ((f32[128,8,128]{2,1,0:T(8,128)}), f32[128,8,128]{2,1,0:T(8,128)S(1)}, u32[]{:S(2)}, u32[]{:S(2)}) async-start(f32[128,8,128]{2,1,0:T(8,128)} %bitcast.9), calls=%async_computation | async-start | bytes 1048576 | tf_op jit(solution)/shard_map/all_to_all | solution.py:488
  80.6 1.9 %collective-permute-start.4 = (f32[2,256,256]{2,1,0:T(8,128)}, f32[2,256,256]{2,1,0:T(8,128)S(1)}, u32[]{:S(2)}, u32[]{:S(2)}) collective-permute-start(f32[2,256,256]{2,1,0:T(8,128)} %get-tuple-element.48), channel_id=1, source_target_pairs={{0,9},{1,10},{2,11},{3,12},{4,13},{5,14},{6,15},{8,17},{9,18},{10,... | collective-permute-start | bytes 1572872 | tf_op jit(solution)/shard_map/ppermute | solution.py:407
  82.5 2.1 %collective-permute-start.5 = (f32[2,256,256]{2,1,0:T(8,128)}, f32[2,256,256]{2,1,0:T(8,128)S(1)}, u32[]{:S(2)}, u32[]{:S(2)}) collective-permute-start(f32[2,256,256]{2,1,0:T(8,128)} %get-tuple-element.49), channel_id=1, source_target_pairs={{0,8},{8,16},{16,24},{24,32},{32,40},{40,48},{48,56},{56,64},{64,7... | collective-permute-start | bytes 1572872 | tf_op jit(solution)/shard_map/ppermute | solution.py:397
  84.6 7.4 %all-to-all-done = f32[128,8,128]{2,1,0:T(8,128)S(1)} async-done(((f32[128,8,128]{2,1,0:T(8,128)}), f32[128,8,128]{2,1,0:T(8,128)S(1)}, u32[]{:S(2)}, u32[]{:S(2)}) %all-to-all-start) | async-done | bytes 524320 | tf_op jit(solution)/shard_map/all_to_all | solution.py:488
  92.0 0.6 broadcast_in_dim.7
  92.7 3.9 %all-to-all-start.1 = ((f32[16,8,128]{2,1,0:T(8,128)}), f32[16,8,128]{2,1,0:T(8,128)S(1)}, u32[]{:S(2)}, u32[]{:S(2)}) async-start(f32[16,8,128]{2,1,0:T(8,128)} %bitcast.3), calls=%async_computation.1 | async-start | bytes 131072 | tf_op jit(solution)/shard_map/all_to_all | solution.py:492
  96.6 3.6 %collective-permute-start.6 = (f32[2,256,256]{2,1,0:T(8,128)}, f32[2,256,256]{2,1,0:T(8,128)S(1)}, u32[]{:S(2)}, u32[]{:S(2)}) collective-permute-start(f32[2,256,256]{2,1,0:T(8,128)} %get-tuple-element.52), channel_id=1, source_target_pairs={{0,8},{8,16},{16,24},{24,32},{32,40},{40,48},{48,56},{56,64},{64,7... | collective-permute-start | bytes 1572872 | tf_op jit(solution)/shard_map/ppermute | solution.py:397
  100.2 0.0 all-to-all-done.1
  100.3 0.0 collective-permute-done.4.across
  100.3 0.0 copy-start.5
  100.3 0.0 collective-permute-done.5.above_left
  100.3 0.0 copy-start.6
  100.3 4.0 %collective-permute-start.7 = (f32[2,256,256]{2,1,0:T(8,128)}, f32[2,256,256]{2,1,0:T(8,128)S(1)}, u32[]{:S(2)}, u32[]{:S(2)}) collective-permute-start(f32[2,256,256]{2,1,0:T(8,128)} %get-tuple-element.54), channel_id=1, source_target_pairs={{0,1},{1,2},{2,3},{3,4},{4,5},{5,6},{6,7},{8,9},{9,10},{10,11},{11... | collective-permute-start | bytes 1572872 | tf_op jit(solution)/shard_map/ppermute | solution.py:397
  104.3 0.9 broadcast_in_dim.8
  105.2 7.2 %all-to-all-start.2 = ((f32[128,8,128]{2,1,0:T(8,128)}), f32[128,8,128]{2,1,0:T(8,128)S(1)}, u32[]{:S(2)}, u32[]{:S(2)}) async-start(f32[128,8,128]{2,1,0:T(8,128)} %bitcast.5), calls=%async_computation.2 | async-start | bytes 1048576 | tf_op jit(solution)/shard_map/all_to_all | solution.py:496
  112.3 0.0 collective-permute-done.6.above_right
  112.3 0.0 copy-start.7
  112.4 0.0 copy-done.4
  112.4 0.0 copy-done.5
  112.4 0.0 copy-done.6
  112.4 0.8 copy-done.7
  113.1 3.7 %shard_map.125.tile = f32[2,512,512]{2,1,0:T(8,128)} custom-call(f32[2,256,256]{2,1,0:T(8,128)} %get-tuple-element.29.top_left, f32[2,256,256]{2,1,0:T(8,128)} %get-tuple-element.33.top_right, f32[2,256,512]{2,1,0:T(8,128)} %get-tuple-element.43.lower, f32[2,256,256]{2,1,0:T(8,128)} %copy-done.4, f32[2,256,256]{2,1,0:T(8,128)} %copy-done.6, ...), custom_call_target="tpu_custom_call" | custom-call | flops 1048576 | bytes 1048576 | tf_op jit(solution)/shard_map/pallas_call | solution.py:447
  116.8 9.6 %all-to-all-done.2 = f32[128,8,128]{2,1,0:T(8,128)S(1)} async-done(((f32[128,8,128]{2,1,0:T(8,128)}), f32[128,8,128]{2,1,0:T(8,128)S(1)}, u32[]{:S(2)}, u32[]{:S(2)}) %all-to-all-start.2) | async-done | bytes 524320 | tf_op jit(solution)/shard_map/all_to_all | solution.py:496
  126.5 0.0 copy-start.2
  126.5 0.0 collective-permute-done.7.left_low
  126.5 0.0 copy-start.9
  126.5 0.8 copy-done.2
  127.3 0.2 copy-done.9
  127.4 2.6 %shard_map.126 = (f32[2,512,512]{2,1,0:T(8,128)}, f32[2,256,256]{2,1,0:T(8,128)}) custom-call(f32[2,512,512]{2,1,0:T(8,128)} %shard_map.125.tile, f32[2,256,256]{2,1,0:T(8,128)} %copy-done.9, f32[2,256,256]{2,1,0:T(8,128)} %probe.1, f32[2,2,256,128]{3,2,1,0:T(8,128)} %bitcast.7), custom_call_target="tpu_custom_call", output_to_operand_aliasing={{0}: (0, {})} | custom-call | flops 1048576 | bytes 1048576 | tf_op jit(solution)/shard_map/pallas_call | solution.py:467
  (3 shorter events, 0.1 us)
Async XLA Ops:
  1.9 28.4 %collective-permute-start = (f32[2,512,256]{2,1,0:T(8,128)S(1)}, f32[2,512,256]{2,1,0:T(8,128)S(1)}, u32[]{:S(2)}, u32[]{:S(2)}) collective-permute-start(f32[2,512,256]{2,1,0:T(8,128)S(1)} %slice.9), channel_id=1, source_target_pairs={{1,0},{2,1},{3,2},{4,3},{5,4},{6,5},{7,6},{9,8},{10,9},{11,10},{12... | collective-permute-start | bytes 3145736 | tf_op jit(solution)/shard_map/ppermute | solution.py:397
  6.0 11.6 %copy-start = (f32[2,512,512]{2,1,0:T(8,128)S(1)}, f32[2,512,512]{2,1,0:T(8,128)}, u32[]{:S(2)}) copy-start(f32[2,512,512]{2,1,0:T(8,128)} %refs_7_.5) | copy-start | bytes 6291460
  17.8 31.0 %collective-permute-start.1 = (f32[2,256,512]{2,1,0:T(8,128)S(1)}, f32[2,256,512]{2,1,0:T(8,128)S(1)}, u32[]{:S(2)}, u32[]{:S(2)}) collective-permute-start(f32[2,256,512]{2,1,0:T(8,128)S(1)} %slice.10), channel_id=1, source_target_pairs={{8,0},{16,8},{24,16},{32,24},{40,32},{48,40},{56,48},{64,56},{72,6... | collective-permute-start | bytes 3145736 | tf_op jit(solution)/shard_map/ppermute | solution.py:397
  20.6 24.6 %collective-permute-start.2 = (f32[2,256,256]{2,1,0:T(8,128)S(1)}, f32[2,256,256]{2,1,0:T(8,128)S(1)}, u32[]{:S(2)}, u32[]{:S(2)}) collective-permute-start(f32[2,256,256]{2,1,0:T(8,128)S(1)} %slice.11), channel_id=1, source_target_pairs={{9,0},{10,1},{11,2},{12,3},{13,4},{14,5},{15,6},{17,8},{18,9},{19,... | collective-permute-start | bytes 1572872 | tf_op jit(solution)/shard_map/ppermute | solution.py:407
  30.3 1.0 copy-start.1
  45.2 8.6 %copy-start.8 = (f32[2,256,256]{2,1,0:T(8,128)}, f32[2,256,256]{2,1,0:T(8,128)S(1)}, u32[]{:S(2)}) copy-start(f32[2,256,256]{2,1,0:T(8,128)S(1)} %collective-permute-done.2.refs_10_) | copy-start | bytes 1572868
  48.8 5.0 %copy-start.3 = (f32[2,256,512]{2,1,0:T(8,128)}, f32[2,256,512]{2,1,0:T(8,128)S(1)}, u32[]{:S(2)}) copy-start(f32[2,256,512]{2,1,0:T(8,128)S(1)} %collective-permute-done.1.refs_8_) | copy-start | bytes 3145732
  48.8 24.2 %collective-permute-start.3 = (f32[2,256,256]{2,1,0:T(8,128)}, f32[2,256,256]{2,1,0:T(8,128)S(1)}, u32[]{:S(2)}, u32[]{:S(2)}) collective-permute-start(f32[2,256,256]{2,1,0:T(8,128)} %get-tuple-element.44), channel_id=1, source_target_pairs={{0,1},{1,2},{2,3},{3,4},{4,5},{5,6},{6,7},{8,9},{9,10},{10,11},{11... | collective-permute-start | bytes 1572872 | tf_op jit(solution)/shard_map/ppermute | solution.py:397
  73.1 39.3 %copy-start.4 = (f32[2,256,256]{2,1,0:T(8,128)}, f32[2,256,256]{2,1,0:T(8,128)S(1)}, u32[]{:S(2)}) copy-start(f32[2,256,256]{2,1,0:T(8,128)S(1)} %collective-permute-done.3.left_top) | copy-start | bytes 1572868
  73.1 18.9 %all-to-all-start = ((f32[128,8,128]{2,1,0:T(8,128)}), f32[128,8,128]{2,1,0:T(8,128)S(1)}, u32[]{:S(2)}, u32[]{:S(2)}) async-start(f32[128,8,128]{2,1,0:T(8,128)} %bitcast.9), calls=%async_computation | async-start | bytes 1048576 | tf_op jit(solution)/shard_map/all_to_all | solution.py:488
  80.6 19.7 %collective-permute-start.4 = (f32[2,256,256]{2,1,0:T(8,128)}, f32[2,256,256]{2,1,0:T(8,128)S(1)}, u32[]{:S(2)}, u32[]{:S(2)}) collective-permute-start(f32[2,256,256]{2,1,0:T(8,128)} %get-tuple-element.48), channel_id=1, source_target_pairs={{0,9},{1,10},{2,11},{3,12},{4,13},{5,14},{6,15},{8,17},{9,18},{10,... | collective-permute-start | bytes 1572872 | tf_op jit(solution)/shard_map/ppermute | solution.py:407
  82.5 17.7 %collective-permute-start.5 = (f32[2,256,256]{2,1,0:T(8,128)}, f32[2,256,256]{2,1,0:T(8,128)S(1)}, u32[]{:S(2)}, u32[]{:S(2)}) collective-permute-start(f32[2,256,256]{2,1,0:T(8,128)} %get-tuple-element.49), channel_id=1, source_target_pairs={{0,8},{8,16},{16,24},{24,32},{32,40},{40,48},{48,56},{56,64},{64,7... | collective-permute-start | bytes 1572872 | tf_op jit(solution)/shard_map/ppermute | solution.py:397
  92.7 7.6 %all-to-all-start.1 = ((f32[16,8,128]{2,1,0:T(8,128)}), f32[16,8,128]{2,1,0:T(8,128)S(1)}, u32[]{:S(2)}, u32[]{:S(2)}) async-start(f32[16,8,128]{2,1,0:T(8,128)} %bitcast.3), calls=%async_computation.1 | async-start | bytes 131072 | tf_op jit(solution)/shard_map/all_to_all | solution.py:492
  96.6 15.7 %collective-permute-start.6 = (f32[2,256,256]{2,1,0:T(8,128)}, f32[2,256,256]{2,1,0:T(8,128)S(1)}, u32[]{:S(2)}, u32[]{:S(2)}) collective-permute-start(f32[2,256,256]{2,1,0:T(8,128)} %get-tuple-element.52), channel_id=1, source_target_pairs={{0,8},{8,16},{16,24},{24,32},{32,40},{40,48},{48,56},{56,64},{64,7... | collective-permute-start | bytes 1572872 | tf_op jit(solution)/shard_map/ppermute | solution.py:397
  100.3 12.1 %copy-start.5 = (f32[2,256,256]{2,1,0:T(8,128)}, f32[2,256,256]{2,1,0:T(8,128)S(1)}, u32[]{:S(2)}) copy-start(f32[2,256,256]{2,1,0:T(8,128)S(1)} %collective-permute-done.4.across) | copy-start | bytes 1572868
  100.3 12.1 %copy-start.6 = (f32[2,256,256]{2,1,0:T(8,128)}, f32[2,256,256]{2,1,0:T(8,128)S(1)}, u32[]{:S(2)}) copy-start(f32[2,256,256]{2,1,0:T(8,128)S(1)} %collective-permute-done.5.above_left) | copy-start | bytes 1572868
  100.3 26.2 %collective-permute-start.7 = (f32[2,256,256]{2,1,0:T(8,128)}, f32[2,256,256]{2,1,0:T(8,128)S(1)}, u32[]{:S(2)}, u32[]{:S(2)}) collective-permute-start(f32[2,256,256]{2,1,0:T(8,128)} %get-tuple-element.54), channel_id=1, source_target_pairs={{0,1},{1,2},{2,3},{3,4},{4,5},{5,6},{6,7},{8,9},{9,10},{10,11},{11... | collective-permute-start | bytes 1572872 | tf_op jit(solution)/shard_map/ppermute | solution.py:397
  105.2 21.3 %all-to-all-start.2 = ((f32[128,8,128]{2,1,0:T(8,128)}), f32[128,8,128]{2,1,0:T(8,128)S(1)}, u32[]{:S(2)}, u32[]{:S(2)}) async-start(f32[128,8,128]{2,1,0:T(8,128)} %bitcast.5), calls=%async_computation.2 | async-start | bytes 1048576 | tf_op jit(solution)/shard_map/all_to_all | solution.py:496
  112.3 0.8 copy-start.7
  126.5 0.8 copy-start.2
  126.5 1.0 copy-start.9
